TPU v7x, 256 devices: a whole 4x4x8 slice. The times are simulated.
256 devices in a mesh: dp: 256 (over y, z, x, core).
Axes of the slice: x: 4, y: 4, z: 8, core: 2. Of those that a mesh axis runs over, the one named last changes fastest.
Arguments:
- features: bfloat16 [256, 1024, 1280], P('dp'), may hold values from -24 to 24
- renoise: bfloat16 [256, 1024, 1280], P('dp'), may hold values from -6 to 6
- critic_grad: bfloat16 [256, 1024, 1280], P('dp'), may hold values from -24 to 24
- student_step: int32 [256], P('dp'), may hold values from 0 to 3
- teacher_step: int32 [256], P('dp'), may hold values from 20 to 979
- student_in: bfloat16 [1280, 640], P('dp'), may hold values from -0.15625 to 0.15625
- student_gain: bfloat16 [1280], P('dp'), may hold values from 0.25 to 1.75
- student_shift: bfloat16 [1280], P('dp'), may hold values from -3 to 3
- student_out: bfloat16 [640, 1280], P(None, 'dp'), may hold values from -0.25 to 0.25
- teacher_in: bfloat16 [1280, 640], P('dp'), may hold values from -0.15625 to 0.15625
- teacher_gain: bfloat16 [1280], P('dp'), may hold values from 0.25 to 1.75
- teacher_shift: bfloat16 [1280], P('dp'), may hold values from -3 to 3
- teacher_out: bfloat16 [640, 1280], P(None, 'dp'), may hold values from -0.25 to 0.25
Outputs:
- grad_in: float32 [1280, 640], P('dp')
- grad_out: float32 [640, 1280], P(None, 'dp')
- grad_gain: float32 [1280], P('dp')
- grad_shift: float32 [1280], P('dp')
All inputs are finite; a program needn't handle non-finite values.
Results may differ from a plain program's by a relative error of at most 0.0014.
Values may be sent and summed in bfloat16 or wider, within the bound.
A program may use at most 128 MiB of HBM per device.

v0:
```python
import math

import jax
import jax.numpy as jnp
from jax import lax
from jax.sharding import PartitionSpec as P

GROUPS = 32
STEPS_T = 1000


EPS = 1e-05


def plan():
    steps = jnp.arange(STEPS_T).astype(jnp.float32)
    lo = math.sqrt(0.00085)
    hi = math.sqrt(0.012)
    betas = (lo + (hi - lo) * steps / (STEPS_T - 1)) ** 2
    return jnp.exp(jnp.cumsum(jnp.log(1.0 - betas)))


def embed(tvals, width):
    half = width // 2
    freqs = jnp.exp(-math.log(10000.0) * jnp.arange(half).astype(jnp.float32) / half)
    angles = tvals[:, None] * freqs[None, :]
    return jnp.concatenate([jnp.cos(angles), jnp.sin(angles)], axis=1)


def group_norm(field):
    batch, rows, chans = field.shape
    width = chans // GROUPS
    count = rows * width
    mean_g = jnp.sum(jnp.sum(field, axis=1).reshape(batch, GROUPS, width), axis=2) / count
    centered = field - jnp.repeat(mean_g, width, axis=1)[:, None, :]
    var_g = (
        jnp.sum(jnp.sum(centered * centered, axis=1).reshape(batch, GROUPS, width), axis=2) / count
    )
    return centered * jnp.repeat(lax.rsqrt(var_g + EPS), width, axis=1)[:, None, :]


def block(field, w_in, gain, shift, w_out, emb):
    batch, rows, chans = field.shape
    normed = group_norm(field)
    hid = (normed * gain.astype(jnp.float32) + shift.astype(jnp.float32)).astype(jnp.bfloat16)
    pre = jnp.dot(hid.reshape(batch * rows, chans), w_in, preferred_element_type=jnp.float32)
    pre = pre.reshape(batch, rows, -1) + emb[:, None, :]
    act = jax.nn.silu(pre).astype(jnp.bfloat16)
    proj = jnp.dot(act.reshape(batch * rows, -1), w_out, preferred_element_type=jnp.float32)
    return (normed, hid, pre, act, field + proj.reshape(batch, rows, chans))


def local(
    features,
    renoise,
    critic_grad,
    student_step,
    teacher_step,
    student_in,
    student_gain,
    student_shift,
    student_out,
    teacher_in,
    teacher_gain,
    teacher_shift,
    teacher_out,
):
    batch, rows, chans = features.shape
    inner = student_in.shape[1]
    ndev = lax.axis_size("dp")
    norm = 1.0 / math.sqrt(rows * batch * ndev)
    s_in, s_gain, s_shift, s_out = (
        lax.all_gather(student_in, "dp", axis=0, tiled=True),
        lax.all_gather(student_gain, "dp", axis=0, tiled=True),
        lax.all_gather(student_shift, "dp", axis=0, tiled=True),
        lax.all_gather(student_out, "dp", axis=1, tiled=True),
    )
    t_in, t_gain, t_shift, t_out = (
        lax.all_gather(teacher_in, "dp", axis=0, tiled=True),
        lax.all_gather(teacher_gain, "dp", axis=0, tiled=True),
        lax.all_gather(teacher_shift, "dp", axis=0, tiled=True),
        lax.all_gather(teacher_out, "dp", axis=1, tiled=True),
    )
    field = features.astype(jnp.float32)
    tval_s = (999 - 250 * student_step).astype(jnp.float32)
    normed, hid, pre, act, sample = block(field, s_in, s_gain, s_shift, s_out, embed(tval_s, inner))
    keep = jnp.sum(
        jnp.where(jnp.arange(STEPS_T)[None, :] == teacher_step[:, None], plan()[None, :], 0.0),
        axis=1,
    )
    keep3 = keep[:, None, None]
    noisy = (jnp.sqrt(keep3) * sample + jnp.sqrt(1.0 - keep3) * renoise.astype(jnp.float32)).astype(
        jnp.bfloat16
    )
    target = block(
        noisy.astype(jnp.float32),
        t_in,
        t_gain,
        t_shift,
        t_out,
        embed(teacher_step.astype(jnp.float32), inner),
    )[4]
    d_sample = ((2.0 * keep3 * (sample - target) + critic_grad.astype(jnp.float32)) * norm).astype(
        jnp.bfloat16
    )
    ds_rows = d_sample.reshape(batch * rows, chans)
    act_rows = act.reshape(batch * rows, inner)
    hid_rows = hid.reshape(batch * rows, chans)
    pre_rows = pre.reshape(batch * rows, inner)
    term_out = lax.dot_general(
        ds_rows, act_rows, (((0,), (0,)), ((), ())), preferred_element_type=jnp.float32
    )
    d_act = lax.dot_general(
        ds_rows, s_out, (((1,), (1,)), ((), ())), preferred_element_type=jnp.float32
    )
    sig = jax.nn.sigmoid(pre_rows)
    d_pre = (d_act * sig * (1.0 + pre_rows * (1.0 - sig))).astype(jnp.bfloat16)
    term_in = lax.dot_general(
        hid_rows, d_pre, (((0,), (0,)), ((), ())), preferred_element_type=jnp.float32
    )
    d_hid = lax.dot_general(
        d_pre, s_in, (((1,), (1,)), ((), ())), preferred_element_type=jnp.float32
    )
    term_gain = jnp.sum(d_hid * normed.reshape(batch * rows, chans), axis=0)
    term_shift = jnp.sum(d_hid, axis=0)
    grad_out_t = lax.psum_scatter(term_out, "dp", scatter_dimension=0, tiled=True)
    grad_in, grad_gain, grad_shift = (
        lax.psum_scatter(term_in, "dp", scatter_dimension=0, tiled=True),
        lax.psum_scatter(term_gain, "dp", scatter_dimension=0, tiled=True),
        lax.psum_scatter(term_shift, "dp", scatter_dimension=0, tiled=True),
    )
    return (grad_in, grad_out_t.T, grad_gain, grad_shift)


def solution(mesh):
    return jax.shard_map(
        local,
        mesh=mesh,
        in_specs=(
            P("dp", None, None),
            P("dp", None, None),
            P("dp", None, None),
            P("dp"),
            P("dp"),
            P("dp", None),
            P("dp"),
            P("dp"),
            P(None, "dp"),
            P("dp", None),
            P("dp"),
            P("dp"),
            P(None, "dp"),
        ),
        out_specs=(P("dp", None), P(None, "dp"), P("dp"), P("dp")),
        check_vma=False,
    )
```

profile of v0, /device:TPU:1, one launch (start us, length us, event | category | flops | bytes accessed | tf_op | source)
XLA Modules:
  0.0 754.8 jit_solution(18396235674231118002)
XLA Ops:
  7.2 0.7 all-gather.9.cloned.1.call-update
  8.0 0.7 all-gather.11.cloned.1.call-update
  8.7 0.7 all-gather.13.cloned.1.call-update
  9.4 0.5 all-gather.15.cloned.1.call-update
  10.1 2.2 convert_reduce_fusion.1
  12.3 0.1 reduce_sum.100
  12.5 0.1 broadcast_in_dim.39
  12.6 0.7 fusion.14
  13.3 0.1 reshape.220
  13.4 0.1 reduce_sum.102
  13.6 0.2 dynamic-update-slice
  13.9 0.2 dynamic-update-slice.1
  14.1 0.2 dynamic-update-slice.2
  14.4 0.2 dynamic-update-slice.3
  14.6 82.2 %all-reduce.11 = (bf16[1280]{0:T(1024)(128)(2,1)S(1)}, bf16[1280]{0:T(1024)(128)(2,1)S(1)}, bf16[1280]{0:T(1024)(128)(2,1)S(1)}, bf16[1280]{0:T(1024)(128)(2,1)S(1)}) all-reduce(bf16[1280]{0:T(1024)(128)(2,1)S(1)} %dynamic-update-slice.1, bf16[1280]{0:T(1024)(128)(2,1)S(1)} %dynamic-update-slice, ...), channel_id=1, replica_groups=mesh['dp'=256] {'dp'}, use_global_device_ids=true, to_apply=%add.2 | all-reduce | flops 5120 | bytes 20480
  96.9 0.1 broadcast_in_dim.41
  97.0 0.3 reduce-window.9
  98.0 0.1 slice_reduce_fusion
  98.2 0.6 select_reduce_fusion
  101.6 0.1 maximum_reduce_fusion
  101.7 0.1 maximum_reduce_fusion.1
  101.8 19.2 %all-gather.9.cloned.1.call-done = bf16[256,5,640]{2,1,0:T(8,128)(2,1)} async-done(((bf16[1,5,640]{2,1,0:T(8,128)(2,1)}), bf16[256,5,640]{2,1,0:T(8,128)(2,1)}) %all-gather.9.cloned.1.call-update) | async-done | bytes 1638416 | tf_op jit(solution)/shard_map/all_gather | solution.py:73
  121.0 4.1 reshape.240
  125.1 103.5 %all-gather.11.cloned.1.call-done = bf16[256,5,640]{2,1,0:T(8,128)(2,1)} async-done(((bf16[1,5,640]{2,1,0:T(8,128)(2,1)}), bf16[256,5,640]{2,1,0:T(8,128)(2,1)}) %all-gather.11.cloned.1.call-update) | async-done | bytes 1638416 | tf_op jit(solution)/shard_map/all_gather | solution.py:76
  228.6 4.1 reshape.242
  232.7 4.1 fusion.35
  236.8 5.0 convert_reduce_fusion
  241.8 0.1 reduce_sum.105
  242.0 0.1 broadcast_in_dim.44
  242.1 2.5 fusion.10
  244.6 0.1 reshape.226
  244.7 0.1 reduce_sum.107
  244.9 0.1 broadcast_in_dim.46
  245.0 91.2 %all-gather.13.cloned.1.call-done = bf16[256,5,640]{2,1,0:T(8,128)(2,1)} async-done(((bf16[1,5,640]{2,1,0:T(8,128)(2,1)}), bf16[256,5,640]{2,1,0:T(8,128)(2,1)}) %all-gather.13.cloned.1.call-update) | async-done | bytes 1638416 | tf_op jit(solution)/shard_map/all_gather | solution.py:79
  336.3 4.1 reshape.244
  340.4 103.4 %all-gather.15.cloned.1.call-done = bf16[256,5,640]{2,1,0:T(8,128)(2,1)} async-done(((bf16[1,5,640]{2,1,0:T(8,128)(2,1)}), bf16[256,5,640]{2,1,0:T(8,128)(2,1)}) %all-gather.15.cloned.1.call-update) | async-done | bytes 1638416 | tf_op jit(solution)/shard_map/all_gather | solution.py:82
  443.8 4.1 reshape.246
  447.8 10.8 %fusion.20 = bf16[1024,1280]{1,0:T(8,128)(2,1)} fusion(bf16[1,1024,1280]{2,1,0:T(8,128)(2,1)} %param.15, f32[1,1024,1280]{2,1,0:T(8,128)} %get-tuple-element.16, bf16[1280,640]{1,0:T(8,128)(2,1)} %reshape.246, bf16[1,1024,1280]{2,1,0:T(8,128)(2,1)} %get-tuple-element.15, f32[]{:T(128)S(6)} %mul.153, bf16[1280,640]{1,0:T(8,128)(2,1)} %reshape.244, ...), kind=kOutput, calls=%fused_computation.27 | convolution fusion | flops 3377725440 | bytes 16407044 | tf_op jit(solution)/shard_map/dot_general | solution.py:49
  458.6 5.7 multiply_convert_fusion
  464.3 4.1 fusion.46
  468.4 4.1 fusion.33
  472.6 4.2 fusion.47
  476.8 77.8 %all-reduce.9 = (f32[1280]{0:T(1024)S(1)}, f32[1280]{0:T(1024)S(1)}) all-reduce(f32[1280]{0:T(1024)S(1)} %get-tuple-element.5, f32[1280]{0:T(1024)S(1)} %get-tuple-element.4), channel_id=4, replica_groups=mesh['dp'=256] {'dp'}, use_global_device_ids=true, to_apply=%region_14.15.clone | all-reduce | flops 2560 | bytes 20480
  554.6 0.6 dynamic-slice.3
  555.2 0.6 dynamic-slice.2
  555.8 189.8 %all-reduce.14.cloned.1.call-done = (f32[1280,640]{1,0:T(8,128)}, f32[1280,640]{1,0:T(8,128)}) async-done(((f32[1280,640]{1,0:T(8,128)}, f32[1280,640]{1,0:T(8,128)}), (f32[1280,640]{1,0:T(8,128)}, f32[1280,640]{1,0:T(8,128)})) %all-reduce.14.cloned.1.call-update) | async-done | bytes 6553616
  745.5 1.4 constant_dynamic-slice_fusion
  746.9 1.4 dynamic-slice_bitcast_fusion
  (53 shorter events, 1.1 us)
Async XLA Ops:
  7.2 5.4 copy-start
  7.2 113.8 %all-gather.9.cloned.1.call-start = ((), (), s32[]{:S(2)}) async-start(), calls=%async_computation | async-start | bytes 2631680 | tf_op jit(solution)/shard_map/all_gather | solution.py:73
  7.9 220.7 %all-gather.11.cloned.1.call-start = ((), (), s32[]{:S(2)}) async-start(), calls=%async_computation.1 | async-start | bytes 2631680 | tf_op jit(solution)/shard_map/all_gather | solution.py:76
  8.7 327.6 %all-gather.13.cloned.1.call-start = ((), (), s32[]{:S(2)}) async-start(), calls=%async_computation.2 | async-start | bytes 2631680 | tf_op jit(solution)/shard_map/all_gather | solution.py:79
  9.4 434.4 %all-gather.15.cloned.1.call-start = ((), (), s32[]{:S(2)}) async-start(), calls=%async_computation.3 | async-start | bytes 2631680 | tf_op jit(solution)/shard_map/all_gather | solution.py:82
  10.0 3.6 copy-start.3
  10.0 3.9 copy-start.4
  10.0 4.1 copy-start.5
  10.0 4.4 copy-start.6
  10.0 735.5 %all-reduce.14.cloned.1.call-start = ((), (), s32[]{:S(2)}) async-start(), calls=%async_computation.4 | async-start | bytes 13107200
  232.7 4.1 copy-start.1
  232.7 4.1 copy-start.2
  236.7 5.0 copy-start.7
  458.6 5.7 copy-start.8
  458.6 5.7 copy-start.9
  464.3 4.1 copy-start.10
Sparse Core Ops, SparseCore 0:
  11.7 109.2 all-gather.8
  124.7 103.8 all-gather.10
  232.3 103.8 all-gather.12
  339.8 103.8 all-gather.14
  472.7 272.7 all-reduce.13
where the time goes:
time: 756 us; the launch traced here: 755 us
  waiting for transfers between devices  510 us (67%)
  blocking collectives  160 us (21%)
  matrix products  37.9 us (5%)
  local copies, waits for them, and re-layouts  22.5 us (3%)
  between operations  17.4 us (2%)
    unnamed x6, waiting for transfers between devices  192 us
    unnamed x2, blocking collectives  160 us
    all_gather x1, waiting for transfers between devices, local(): lax.all_gather(student_out, 'dp', axis=1, tiled=True)  104 us
    all_gather x1, waiting for transfers between devices, local(): lax.all_gather(teacher_out, 'dp', axis=1, tiled=True)  103 us
    all_gather x1, waiting for transfers between devices, local(): lax.all_gather(teacher_in, 'dp', axis=0, tiled=True)  91.2 us
    unnamed x37, local copies, waits for them, and re-layouts  20 us
    all_gather x1, waiting for transfers between devices, local(): lax.all_gather(student_in, 'dp', axis=0, tiled=True)  19.2 us
    dot_general x2, matrix products, block(): jnp.dot(act.reshape(batch * rows, -1), w_out, preferred_element_type=jnp....  15.8 us
  transfers between devices with their start and end apart: 5, of which 5 were waited for; matrix products, arithmetic and copies ran while one was open for 5% of the time, Pallas kernels for 0%

commit v1 on v0

v1 whole, which is shorter than its diff:
```python
import functools
import math

import jax
import jax.numpy as jnp
import numpy as np
from jax import lax
from jax.experimental import pallas as pl
from jax.experimental.pallas import tpu as pltpu
from jax.sharding import PartitionSpec as P

GROUPS = 32
STEPS_T = 1000
EPS = 1e-05
MESH = pl.DeviceIdType.MESH
F32 = jnp.float32
BF16 = jnp.bfloat16


def keep_of(step):
    steps = jnp.arange(STEPS_T).astype(F32)
    lo = math.sqrt(0.00085)
    hi = math.sqrt(0.012)
    betas = (lo + (hi - lo) * steps / (STEPS_T - 1)) ** 2
    logs = jnp.log(1.0 - betas)
    return jnp.exp(jnp.sum(jnp.where(jnp.arange(STEPS_T) <= step, logs, 0.0)))


def embed(tval, width):
    half = width // 2
    freqs = jnp.exp(-math.log(10000.0) * jnp.arange(half).astype(F32) / half)
    angles = tval * freqs
    return jnp.concatenate([jnp.cos(angles), jnp.sin(angles)])[None, :]


def dev(y, z, x, c):
    return ((y * 8 + z) * 4 + x) * 2 + c


def where_am_i():
    me = lax.axis_index("dp")
    c = lax.rem(me, 2)
    x = lax.rem(lax.div(me, 2), 4)
    z = lax.rem(lax.div(me, 8), 8)
    y = lax.div(me, 64)
    return y, z, x, c


class Ring:
    def __init__(self, b, y, z, x, c):
        r = lax.rem(c + b, 2)
        self.r = r
        self.p = (1 - r) * y + r * x
        self.q = (1 - r) * x + r * y
        self.at = (y, z, x, c)

    def block(self, dp, dq):
        pp = lax.rem(self.p + dp, 4)
        qq = lax.rem(self.q + dq, 4)
        return pp * (4 - 3 * self.r) + qq * (1 + 3 * self.r)

    def first(self, d):
        y, z, x, c = self.at
        r = self.r
        return dev(lax.rem(y + (1 - r) * d, 4), z, lax.rem(x + r * d, 4), c)

    def second(self, d):
        y, z, x, c = self.at
        r = self.r
        return dev(lax.rem(y + r * d, 4), z, lax.rem(x + (1 - r) * d, 4), c)


def signal(device):
    pl.semaphore_signal(pltpu.get_barrier_semaphore(), inc=1, device_id=(device,), device_id_type=MESH)


def remote(src, dst, ssem, rsem, device):
    return pltpu.make_async_remote_copy(
        src_ref=src, dst_ref=dst, send_sem=ssem, recv_sem=rsem, device_id=(device,), device_id_type=MESH
    )


def greet_planes(y, z, x, c):
    for d in (1, 3):
        signal(dev(y, z, lax.rem(x + d, 4), c))
        signal(dev(lax.rem(y + d, 4), z, x, c))
    signal(dev(y, z, x, 1 - c))


def gather_kernel(raw_ref, sel_ref, w_ref, vec_ref, rbuf, wb, r_send, r_recv, s_send, s_recv, s_sib):
    y, z, x, c = where_am_i()
    mine = lax.div(z, 2) == x
    greet_planes(y, z, x, c)
    for k in range(1, 16):
        signal(dev(y, 2 * x + lax.rem(z + k // 8, 2), lax.rem(x + k // 2, 4), lax.rem(c + k, 2)))

    @pl.when(jnp.logical_not(mine))
    def _():
        signal(dev(y, 2 * x + lax.rem(z, 2), x, c))

    pl.semaphore_wait(pltpu.get_barrier_semaphore(), jnp.where(mine, 20, 21))

    slot = lax.rem(z, 2) * 8 + x * 2 + c
    to_x = lax.div(z, 2)
    own = pltpu.make_async_copy(raw_ref.at[c], rbuf.at[slot], r_recv)
    for k in range(1, 16):
        cc = lax.rem(c + k, 2)
        remote(
            raw_ref.at[cc], rbuf.at[slot], r_send, r_recv, dev(y, lax.rem(z + k // 2, 8), to_x, cc)
        ).start()
    first = remote(raw_ref.at[c], rbuf.at[slot], r_send, r_recv, dev(y, z, to_x, c))

    @pl.when(mine)
    def _():
        own.start()

    @pl.when(jnp.logical_not(mine))
    def _():
        first.start()

    pltpu.make_async_copy(rbuf, rbuf, r_recv).wait()

    rings = [Ring(b, y, z, x, c) for b in range(2)]

    def at(b, g, core=None):
        return wb.at[(b * 2 + (c if core is None else core)) * 16 + g]

    def send(b, g, device):
        remote(at(b, g), at(b, g), s_send.at[b], s_recv.at[b, g], device).start()

    def to_sibling(b, g):
        remote(at(b, g), at(b, g), s_send.at[b], s_sib.at[b], dev(y, z, x, 1 - c)).start()

    def wait(b, g):
        remote(at(b, g), at(b, g), s_send.at[b], s_recv.at[b, g], dev(y, z, x, 1 - c)).wait_recv()

    row = lax.broadcasted_iota(jnp.int32, (16, 128), 0)
    for b in range(2):
        ring = rings[b]
        g = ring.block(0, 0)
        k = (b * 2 + c) * 16 + g
        outs = []
        for h in range(2):
            t = 2 * b + h
            raw = rbuf[:, 16 * t : 16 * t + 16, :].reshape(256, 128)
            out = jnp.dot(sel_ref[...], raw, preferred_element_type=F32)
            outs.append(out[240:256])
            for i in range(3):
                j = 3 * h + i
                if j < 5:
                    wb[k, 80 * j : 80 * j + 80, :] = out[80 * i : 80 * i + 80].astype(BF16)
        wb[k, 400:416, :] = jnp.where(row == 0, outs[0], outs[1]).astype(BF16)
        send(b, g, ring.first(1))
        send(b, g, ring.first(3))
        send(b, g, ring.second(1))
        send(b, g, ring.second(3))
        to_sibling(b, g)

    for b in range(2):
        ring = rings[b]
        for d in (3, 1, 2):
            g = ring.block(d, 0)
            wait(b, g)
            if d == (3 if b == 0 else 1):
                send(b, g, ring.first(1 if b == 0 else 3))
            send(b, g, ring.second(1))
            send(b, g, ring.second(3))
            to_sibling(b, g)
        for n, d in enumerate((0, 3, 1, 2)):
            for e in (3, 1):
                g = ring.block(d, e)
                wait(b, g)
                if e == (3 if n % 2 == 0 else 1):
                    send(b, g, ring.second(1 if e == 3 else 3))
                to_sibling(b, g)
        for d in (0, 3, 1, 2):
            g = ring.block(d, 2)
            wait(b, g)
            to_sibling(b, g)

    for b in range(2):
        pltpu.make_async_copy(wb.at[pl.ds(0, 16)], wb.at[pl.ds(0, 16)], s_sib.at[b]).wait()
    for b in range(2):
        pltpu.make_async_copy(wb.at[pl.ds(0, 31)], wb.at[pl.ds(0, 31)], s_send.at[b]).wait()
    @pl.when(mine)
    def _():
        pltpu.make_async_copy(rbuf.at[pl.ds(0, 15)], rbuf.at[pl.ds(0, 15)], r_send).wait()

    @pl.when(jnp.logical_not(mine))
    def _():
        pltpu.make_async_copy(rbuf, rbuf, r_send).wait()

    for n in range(4):
        for j in range(5):
            w_ref[n, :, 128 * j : 128 * j + 128] = wb[16 * n : 16 * n + 16, 80 * j : 80 * j + 80, :].reshape(1280, 128)
    lane = lax.broadcasted_iota(jnp.int32, (16, 128), 1)
    for b in range(2):
        acc = [jnp.zeros((16, 128), F32) for _ in range(10)]
        for g in range(16):
            block, s = divmod(80 * g, 128)
            v = wb[2 * b * 16 + g, 400:416, :].astype(F32)
            if s:
                v = pltpu.roll(v, s, 1)
            acc[block] += jnp.where(lane >= s, v, 0.0)
            if s + 80 > 128:
                acc[block + 1] += jnp.where(lane < s, v, 0.0)
        for n in range(10):
            vec_ref[b, :, 128 * n : 128 * n + 128] = acc[n]


def selection():
    sel = np.zeros((256, 256), np.float32)
    for m in range(240):
        i, q = divmod(m, 80)
        sel[m, 16 * (q // 5) + 5 * i + q % 5] = 1.0
    for d in range(16):
        sel[240:242, 16 * d + 15] = 1.0
    return jnp.asarray(sel, BF16)


def packed(student, teacher, vectors):
    tiles = []
    for shard, (gain, shift) in ((student, vectors[0]), (teacher, vectors[1])):
        slabs = shard.reshape(5, 5, 128).transpose(1, 0, 2).reshape(25, 128)
        tiles += [slabs[:15], gain, slabs[15:], jnp.zeros((5, 128), BF16), shift]
    return jnp.concatenate(tiles)


def gather(student_in, student_gain, student_shift, student_out, teacher_in, teacher_gain, teacher_shift, teacher_out):
    place = 5 * lax.rem(lax.axis_index("dp"), 16)

    def spread(v):
        return lax.dynamic_update_slice(jnp.zeros((1, 128), BF16), v[None, :], (0, place))

    vectors = ((spread(student_gain), spread(student_shift)), (spread(teacher_gain), spread(teacher_shift)))
    raw = jnp.stack([packed(student_in, teacher_in, vectors), packed(student_out.T, teacher_out.T, vectors)])
    vmem = pl.BlockSpec(memory_space=pltpu.VMEM)
    return pl.pallas_call(
        gather_kernel,
        out_shape=(jax.ShapeDtypeStruct((4, 1280, 640), BF16), jax.ShapeDtypeStruct((2, 16, 1280), F32)),
        in_specs=[vmem, vmem],
        out_specs=(vmem, vmem),
        scratch_shapes=[
            pltpu.VMEM((16, 64, 128), BF16),
            pltpu.VMEM((64, 416, 128), BF16),
            pltpu.SemaphoreType.DMA,
            pltpu.SemaphoreType.DMA,
            pltpu.SemaphoreType.DMA((2,)),
            pltpu.SemaphoreType.DMA((2, 16)),
            pltpu.SemaphoreType.DMA((2,)),
        ],
        compiler_params=pltpu.CompilerParams(collective_id=0, has_side_effects=True, vmem_limit_bytes=48 * 2**20),
    )(raw, selection())


def scatter_kernel(
    g_ref, o_ref, sib, t1, fm, fp, acc, u1, um, up, stage, fin,
    h_send, h_recv, q_send, t_recv, m_recv, p_recv, p_send, ut_recv, um_recv, up_recv, f_send, f_recv,
):
    y, z, x, c = where_am_i()
    selfish = (2 * x + c) == z
    greet_planes(y, z, x, c)
    from_x, from_c = lax.div(z, 2), lax.rem(z, 2)
    for k in range(1, 8):
        signal(dev(y, lax.rem(z + k, 8), from_x, from_c))

    @pl.when(jnp.logical_not(selfish))
    def _():
        signal(dev(y, z, from_x, from_c))

    pl.semaphore_wait(pltpu.get_barrier_semaphore(), jnp.where(selfish, 12, 13))

    rings = [Ring(b, y, z, x, c) for b in range(2)]
    order = [(d, 2) for d in (2, 1, 3, 0)] + [(d, e) for d in (2, 1, 3, 0) for e in (1, 3)] + [(d, 0) for d in (2, 1, 3, 0)]

    def to_sibling(b, g):
        return remote(g_ref.at[b, g, 1 - c], sib.at[b, g], h_send.at[b], h_recv.at[b, g], dev(y, z, x, 1 - c))

    for b in range(2):
        other = Ring(b + 1, y, z, x, c)
        for d, e in order:
            to_sibling(b, other.block(d, e)).start()

    def meet(b, g):
        to_sibling(b, g).wait_recv()
        sib[b, g] += g_ref[b, g, c]

    for b in range(2):
        ring = rings[b]

        def push(g, dst, recv, d):
            remote(sib.at[b, g], dst, q_send.at[b], recv, ring.second(d)).start()

        for k in range(4):
            d = (2, 1, 3, 0)[k]
            g = ring.block(d, 2)
            meet(b, g)
            push(g, t1.at[b, k], t_recv.at[b, k], 1 if k % 2 == 0 else 3)
        for k in range(4):
            d = (2, 1, 3, 0)[k]
            for e in (3, 1) if k % 2 == 0 else (1, 3):
                g = ring.block(d, e)
                meet(b, g)
                if e == (1 if k % 2 == 0 else 3):
                    remote(t1.at[b, k], t1.at[b, k], q_send.at[b], t_recv.at[b, k], ring.second(1)).wait_recv()
                    sib[b, g] += t1[b, k]
                if e == 1:
                    push(g, fm.at[b, k], m_recv.at[b, k], 1)
                else:
                    push(g, fp.at[b, k], p_recv.at[b, k], 3)

    for b in range(2):
        ring = rings[b]

        def push1(k, dst, recv, d):
            remote(acc.at[b, k], dst, p_send.at[b], recv, ring.first(d)).start()

        def arrive(dst, recv):
            remote(dst, dst, p_send.at[b], recv, ring.first(1)).wait_recv()

        for k in range(4):
            d = (2, 1, 3, 0)[k] if b == 0 else (2, 3, 1, 0)[k]
            kk = (2, 1, 3, 0).index(d)
            g = ring.block(d, 0)
            meet(b, g)
            arrive(fm.at[b, kk], m_recv.at[b, kk])
            arrive(fp.at[b, kk], p_recv.at[b, kk])
            acc[b, k] = sib[b, g] + fm[b, kk] + fp[b, kk]
            if k == 0:
                push1(k, u1.at[b], ut_recv.at[b], 1 if b == 0 else 3)
            if k == 1:
                arrive(u1.at[b], ut_recv.at[b])
                acc[b, k] += u1[b]
            if k in (1, 2):
                if d == 1:
                    push1(k, um.at[b], um_recv.at[b], 1)
                else:
                    push1(k, up.at[b], up_recv.at[b], 3)
        arrive(um.at[b], um_recv.at[b])
        arrive(up.at[b], up_recv.at[b])
        total = acc[b, 3] + um[b] + up[b]
        for s in range(8):
            for j in range(5):
                stage[b, s, 0:5, 128 * j : 128 * j + 128] = total[40 * j + 5 * s : 40 * j + 5 * s + 5]
            v = total[200:208]
            if s:
                v = pltpu.roll(v, 128 - 5 * s, 1)
            stage[b, s, 5:7, 0:128] = v[0:2]
        for k in range(1, 8):
            s = lax.rem(x * 2 + c + k, 8)
            remote(
                stage.at[b, s], fin.at[b, z], f_send.at[b], f_recv.at[b],
                dev(y, 2 * x + c, lax.div(s, 2), lax.rem(s, 2)),
            ).start()
        s = x * 2 + c
        own = pltpu.make_async_copy(stage.at[b, s], fin.at[b, z], f_recv.at[b])
        far = remote(stage.at[b, s], fin.at[b, z], f_send.at[b], f_recv.at[b], dev(y, 2 * x + c, x, c))

        @pl.when(selfish)
        def _():
            own.start()

        @pl.when(jnp.logical_not(selfish))
        def _():
            far.start()

    for b in range(2):
        pltpu.make_async_copy(fin.at[b], fin.at[b], f_recv.at[b]).wait()
        o_ref[b] = jnp.sum(fin[b], axis=0)
    for b in range(2):
        pltpu.make_async_copy(sib.at[b], sib.at[b], h_send.at[b]).wait()
        pltpu.make_async_copy(sib.at[b, pl.ds(0, 12)], sib.at[b, pl.ds(0, 12)], q_send.at[b]).wait()
        pltpu.make_async_copy(acc.at[b, pl.ds(0, 3)], acc.at[b, pl.ds(0, 3)], p_send.at[b]).wait()

        @pl.when(selfish)
        def _():
            pltpu.make_async_copy(fin.at[b, pl.ds(0, 7)], fin.at[b, pl.ds(0, 7)], f_send.at[b]).wait()

        @pl.when(jnp.logical_not(selfish))
        def _():
            pltpu.make_async_copy(fin.at[b], fin.at[b], f_send.at[b]).wait()


def scatter(grads):
    vmem = pl.BlockSpec(memory_space=pltpu.VMEM)
    block = (208, 128)
    dma = pltpu.SemaphoreType.DMA
    return pl.pallas_call(
        scatter_kernel,
        out_shape=jax.ShapeDtypeStruct((2, 8, 640), F32),
        in_specs=[vmem],
        out_specs=vmem,
        scratch_shapes=[
            pltpu.VMEM((2, 16, *block), F32),
            pltpu.VMEM((2, 4, *block), F32),
            pltpu.VMEM((2, 4, *block), F32),
            pltpu.VMEM((2, 4, *block), F32),
            pltpu.VMEM((2, 4, *block), F32),
            pltpu.VMEM((2, *block), F32),
            pltpu.VMEM((2, *block), F32),
            pltpu.VMEM((2, *block), F32),
            pltpu.VMEM((2, 8, 8, 640), F32),
            pltpu.VMEM((2, 8, 8, 640), F32),
            dma((2,)),
            dma((2, 16)),
            dma((2,)),
            dma((2, 4)),
            dma((2, 4)),
            dma((2, 4)),
            dma((2,)),
            dma((2,)),
            dma((2,)),
            dma((2,)),
            dma((2,)),
            dma((2,)),
        ],
        compiler_params=pltpu.CompilerParams(collective_id=1, has_side_effects=True, vmem_limit_bytes=48 * 2**20),
    )(grads)


def group_norm(field):
    rows, chans = field.shape
    width = chans // GROUPS
    count = rows * width
    mean_g = jnp.sum(jnp.sum(field, axis=0).reshape(GROUPS, width), axis=1) / count
    centered = field - jnp.repeat(mean_g, width)[None, :]
    var_g = jnp.sum(jnp.sum(centered * centered, axis=0).reshape(GROUPS, width), axis=1) / count
    return centered * jnp.repeat(lax.rsqrt(var_g + EPS), width)[None, :]


def block(field, w_in, gain, shift, w_out_t, emb):
    normed = group_norm(field)
    hid = (normed * gain + shift).astype(BF16)
    pre = jnp.dot(hid, w_in, preferred_element_type=F32) + emb
    act = jax.nn.silu(pre).astype(BF16)
    proj = lax.dot_general(act, w_out_t, (((1,), (1,)), ((), ())), preferred_element_type=F32)
    return normed, hid, pre, act, field + proj


def local(
    features,
    renoise,
    critic_grad,
    student_step,
    teacher_step,
    student_in,
    student_gain,
    student_shift,
    student_out,
    teacher_in,
    teacher_gain,
    teacher_shift,
    teacher_out,
):
    rows, chans = features.shape[1:]
    inner = student_in.shape[1]
    norm = 1.0 / math.sqrt(rows * lax.axis_size("dp"))
    w, vec = gather(
        student_in, student_gain, student_shift, student_out, teacher_in, teacher_gain, teacher_shift, teacher_out
    )
    field = features[0].astype(F32)
    tval_s = (999 - 250 * student_step[0]).astype(F32)
    normed, hid, pre, act, sample = block(field, w[0], vec[0, 0:1], vec[0, 1:2], w[1], embed(tval_s, inner))
    keep = keep_of(teacher_step[0])
    noisy = (jnp.sqrt(keep) * sample + jnp.sqrt(1.0 - keep) * renoise[0].astype(F32)).astype(BF16)
    target = block(
        noisy.astype(F32), w[2], vec[1, 0:1], vec[1, 1:2], w[3], embed(teacher_step[0].astype(F32), inner)
    )[4]
    d_sample = ((2.0 * keep * (sample - target) + critic_grad[0].astype(F32)) * norm).astype(BF16)
    rows_of = (((0,), (0,)), ((), ()))
    term_out = lax.dot_general(d_sample, act, rows_of, preferred_element_type=F32)
    d_act = jnp.dot(d_sample, w[1], preferred_element_type=F32)
    sig = jax.nn.sigmoid(pre)
    d_pre = (d_act * sig * (1.0 + pre * (1.0 - sig))).astype(BF16)
    term_in = lax.dot_general(hid, d_pre, rows_of, preferred_element_type=F32)
    d_hid = lax.dot_general(d_pre, w[0], (((1,), (1,)), ((), ())), preferred_element_type=F32)
    vecs = jnp.stack([jnp.sum(d_hid * normed, axis=0), jnp.sum(d_hid, axis=0)])
    vecs = jnp.pad(vecs.reshape(2, 32, 40).transpose(1, 0, 2), ((0, 0), (0, 6), (0, 88)))
    slabs = jnp.stack([term_out, term_in]).reshape(2, 32, 40, 5, 128).transpose(0, 1, 3, 2, 4).reshape(2, 32, 200, 128)
    grads = jnp.concatenate([slabs, jnp.broadcast_to(vecs, (2, 32, 8, 128))], axis=2).reshape(2, 16, 2, 208, 128)
    out = scatter(grads)
    return out[1, :5], out[0, :5].T, out[1, 5, :5], out[1, 6, :5]


def solution(mesh):
    return jax.shard_map(
        local,
        mesh=mesh,
        in_specs=(
            P("dp", None, None),
            P("dp", None, None),
            P("dp", None, None),
            P("dp"),
            P("dp"),
            P("dp", None),
            P("dp"),
            P("dp"),
            P(None, "dp"),
            P("dp", None),
            P("dp"),
            P("dp"),
            P(None, "dp"),
        ),
        out_specs=(P("dp", None), P(None, "dp"), P("dp"), P("dp")),
        check_vma=False,
    )
```

time: 756 us -> 195 us (0.26)
  waiting for transfers between devices: 510 us -> 0 us
  blocking collectives: 160 us -> 0 us
  Pallas kernels: 0 us -> 109 us
  between operations: 17.4 us -> 3.13 us
    all_gather x4 -> x0, waiting for transfers between devices: 317 us -> none  [the longest x1 104 us: local(): lax.all_gather(student_out, 'dp', axis=1, tiled=True)]
    unnamed x6 -> x0, waiting for transfers between devices: 192 us -> none
    unnamed x2 -> x0, blocking collectives: 160 us -> none
    pallas_call x0 -> x2, Pallas kernels: none -> 109 us  [the longest x1 55.1 us: gather(): pl.pallas_call(gather_kernel, out_shape=(jax.ShapeDtypeStruct((4, 1280, 6...]
    unnamed x37 -> x12, local copies, waits for them, and re-layouts: 20 us -> 0.03 us
    another operation x1 -> x9, local copies, waits for them, and re-layouts: 0.11 us -> 8.14 us  [the longest x2 7.95 us: local(): jnp.stack([term_out, term_in]).reshape(2, 32, 40, 5, 128)]
  transfers between devices with their start and end apart: 5 -> 0, of which waited for: 5 -> 0; matrix products, arithmetic and copies ran while one was open for 5% -> 0% of each run, Pallas kernels for 0% -> 0%
where the time goes in v1:
time: 195 us; the launch traced here: 193 us
  Pallas kernels  109 us (56%)
  matrix products  45.1 us (23%)
  local copies, waits for them, and re-layouts  24.3 us (12%)
  other arithmetic  11.3 us (6%)
  between operations  3.13 us (2%)
    pallas_call x1, Pallas kernels, gather(): pl.pallas_call(gather_kernel, out_shape=(jax.ShapeDtypeStruct((4, 1280, 6...  55.1 us
    pallas_call x1, Pallas kernels, scatter(): pl.pallas_call(scatter_kernel, out_shape=jax.ShapeDtypeStruct((2, 8, 640)...  53.7 us
    dot_general x2, matrix products, block(): lax.dot_general(act, w_out_t, (((1,), (1,)), ((), ())), preferred_element...  18.8 us
    another operation x2, local copies, waits for them, and re-layouts, local(): jnp.stack([term_out, term_in]).reshape(2, 32, 40, 5, 128)  7.95 us
    dot_general x1, matrix products, local(): lax.dot_general(d_sample, act, rows_of, preferred_element_type=F32)  6.91 us
    dot_general x1, matrix products, local(): lax.dot_general(d_pre, w[0], (((1,), (1,)), ((), ())), preferred_element_...  6.21 us
    slice x16, local copies, waits for them, and re-layouts, packed(): tiles += [slabs[:15], gain, slabs[15:], jnp.zeros((5, 128), BF16), shift]  5.61 us
    dot_general x1, matrix products, local(): d_act = jnp.dot(d_sample, w[1], preferred_element_type=F32)  5.19 us

profile of v1, /device:TPU:1, one launch (start us, length us, event | category | flops | bytes accessed | tf_op | source)
XLA Modules:
  0.0 192.6 jit_solution(1112554556233408036)
XLA Ops:
  1.4 0.6 select_reduce_fusion
  3.5 0.9 dynamic_update_slice.14
  4.4 0.9 dynamic_update_slice.13
  5.2 0.9 dynamic_update_slice.12
  6.1 0.9 dynamic_update_slice.15
  7.2 0.7 slice.115
  8.0 0.7 slice.119
  8.7 0.7 slice.117
  9.4 0.7 slice.121
  10.1 0.7 slice.114
  10.8 0.7 slice.118
  11.5 0.7 slice.116
  12.2 0.2 concatenate.20
  12.3 0.7 slice.120
  13.1 0.2 concatenate.21
  13.2 2.2 %convert_reduce_fusion.1 = f32[1280]{0:T(1024)S(1)} fusion(bf16[1,1024,1280]{2,1,0:T(8,128)(2,1)} %param.14), kind=kLoop, calls=%fused_computation.4 | loop fusion | flops 2620160 | bytes 2626560 | tf_op jit(solution)/shard_map/reduce_sum | solution.py:425
  15.4 0.1 reshape.113
  15.5 0.1 reduce_sum.101
  15.7 0.1 sub.49
  15.8 0.7 fusion.15
  16.6 0.1 reshape.114
  16.6 0.1 reduce_sum.103
  16.8 0.1 mul.129
  17.0 55.1 %shard_map.165 = (bf16[4,1280,640]{2,1,0:T(8,128)(2,1)}, f32[2,16,1280]{2,1,0:T(8,128)S(1)}) custom-call(bf16[2,64,128]{2,1,0:T(8,128)(2,1)S(1)} %pad_maximum_fusion.2.raw_ref, bf16[256,256]{1,0:T(8,128)(2,1)S(1)} %copy-done), custom_call_target="tpu_custom_call" | custom-call | tf_op jit(solution)/shard_map/pallas_call | solution.py:238
  72.2 3.6 %fusion.27 = f32[1024,640]{0,1:T(8,128)S(1)} fusion(bf16[1,1024,1280]{2,1,0:T(8,128)(2,1)S(1)} %copy-done.1, f32[1280]{0:T(1024)S(1)} %get-tuple-element.12, f32[1280]{0:T(1024)S(1)} %get-tuple-element.13, f32[1280]{0:T(1024)S(1)} %mul.129, f32[1280]{0:T(1024)S(1)} %sub.49, bf16[4,1280,640]{2,1,0:T(8,128)(2,1)} %get-tuple-element.7), kind=kOutput, calls=%fused_computation.36 | convolution fusion | flops 1685585920 | bytes 6901760 | tf_op jit(solution)/shard_map/dot_general | solution.py:434
  75.8 7.8 %convert_reduce_fusion = (f32[1280]{0:T(1024)S(1)}, bf16[1024,1280]{1,0:T(8,128)(2,1)}, f32[1024,1280]{1,0:T(8,128)}) fusion(bf16[1,1024,1280]{2,1,0:T(8,128)(2,1)S(1)} %copy-done.2, f32[]{:T(128)S(6)} %sqrt.7, f32[]{:T(128)S(6)} %sqrt.6, bf16[4,1280,640]{2,1,0:T(8,128)(2,1)} %get-tuple-element.7, f32[1024,640]{0,1:T(8,128)S(1)} %fusion.27, ...), kind=kOutput, calls=%fused_computation.2 | convolution fusion | flops 1693448960 | bytes 17374728 | tf_op jit(solution)/shard_map/dot_general | solution.py:436
  83.5 0.1 reshape.119
  83.6 0.1 reduce_sum.105
  83.8 0.1 sub.56
  83.9 2.5 %fusion.11 = f32[1280]{0:T(1024)S(1)} fusion(bf16[1024,1280]{1,0:T(8,128)(2,1)} %get-tuple-element.15, f32[1280]{0:T(1024)S(1)} %sub.56), kind=kLoop, calls=%fused_computation.19 | loop fusion | flops 5241600 | bytes 2631680 | tf_op jit(solution)/shard_map/reduce_sum | solution.py:427
  86.4 0.1 reshape.120
  86.5 0.1 reduce_sum.107
  86.7 0.1 mul.144
  86.8 11.0 %fusion.24 = bf16[1024,1280]{1,0:T(8,128)(2,1)} fusion(f32[1024,1280]{1,0:T(8,128)} %get-tuple-element.21, bf16[1024,1280]{1,0:T(8,128)(2,1)} %get-tuple-element.15, bf16[1,1024,1280]{2,1,0:T(8,128)(2,1)} %param.16, f32[]{:T(128)S(6)} %mul_shard_map.10, bf16[4,1280,640]{2,1,0:T(8,128)(2,1)} %get-tuple-element.7, f32[1280]{0:T(1024)S(1)} %get-tuple-element.11, ...), kind=kOutput, calls=%fused_computation.32 | convolution fusion | flops 3377725440 | bytes 19028484 | tf_op jit(solution)/shard_map/dot_general | solution.py:436
  97.8 6.9 %fusion.79 = f32[1280,640]{1,0:T(8,128)} fusion(bf16[1024,1280]{1,0:T(8,128)(2,1)} %fusion.24, f32[1024,640]{0,1:T(8,128)} %copy-done.3, f32[640]{0:T(1024)S(1)} %pad_maximum_fusion.3), kind=kOutput, calls=%fused_computation.105 | convolution fusion | flops 1681653760 | bytes 8522240 | tf_op jit(solution)/shard_map/dot_general | solution.py:471
  104.7 5.2 %fusion.37 = (bf16[640,1024]{1,0:T(8,128)(2,1)}, f32[1024,640]{0,1:T(8,128)S(1)}) fusion(f32[1024,640]{0,1:T(8,128)S(1)} %copy-done.4, f32[640]{0:T(1024)S(1)} %pad_maximum_fusion.3, bf16[1024,1280]{1,0:T(8,128)(2,1)S(1)} %copy-done.5, bf16[4,1280,640]{2,1,0:T(8,128)(2,1)} %get-tuple-element.7), kind=kOutput, calls=%fused_computation.46 | convolution fusion | flops 1684275200 | bytes 10816000 | tf_op jit(solution)/shard_map/dot_general | solution.py:472
  109.9 6.2 %fusion.10 = (f32[1280]{0:T(1024)S(1)}, f32[1280]{0:T(1024)S(1)}, bf16[1280,1024]{0,1:T(8,128)(2,1)}) fusion(bf16[1,1024,1280]{2,1,0:T(8,128)(2,1)S(1)} %copy-done.1, f32[1280]{0:T(1024)S(1)} %mul.129, f32[1280]{0:T(1024)S(1)} %sub.49, f32[1280]{0:T(1024)S(1)} %get-tuple-element.12, f32[1280]{0:T(1024)S(1)} %get-tuple-element.13, ...), kind=kOutput, calls=%fused_computation.18 | convolution fusion | flops 1696069120 | bytes 12157440 | tf_op jit(solution)/shard_map/dot_general | solution.py:476
  116.2 0.1 stack.30
  116.3 0.1 stack.31
  116.4 4.9 %stack.28 = f32[1,32,40,5,128]{4,3,2,1,0:T(8,128)} reshape(f32[1280,640]{1,0:T(8,128)} %fusion.79) | data formatting | bytes 6553600 | tf_op jit(solution)/shard_map/stack | solution.py:479
  121.3 3.1 %copy.38 = f32[1,32,40,5,128]{4,2,3,1,0:T(8,128)S(1)} copy(f32[1,32,40,5,128]{4,3,2,1,0:T(8,128)} %stack.28) | data formatting | bytes 6553600 | tf_op jit(solution)/shard_map/stack | solution.py:479
  124.4 4.5 %copy.37 = bf16[1280,1024]{1,0:T(8,128)(2,1)} copy(bf16[1280,1024]{0,1:T(8,128)(2,1)} %get-tuple-element.16) | data formatting | bytes 5242880 | tf_op jit(solution)/shard_map/dot_general | solution.py:475
  128.9 4.4 %convolution_bitcast_fusion = f32[1,32,40,5,128]{4,2,3,1,0:T(8,128)S(1)} fusion(bf16[32,40,1024,1]{2,1,3,0:T(8,128)(2,1)} %bitcast.141, bf16[5,128,1024,1]{2,1,0,3:T(8,128)(2,1)} %bitcast.157), kind=kOutput, calls=%fused_computation.60 | convolution fusion | flops 1677721600 | bytes 7208960 | tf_op jit(solution)/shard_map/dot_general | solution.py:475
  133.3 0.8 pad_maximum_fusion.1
  134.2 3.6 %pad_maximum_fusion.g_ref = f32[2,16,2,208,128]{4,3,2,1,0:T(8,128)} fusion(f32[2,16,2,8,128]{4,3,2,1,0:T(8,128)S(1)} %broadcast_in_dim.45, f32[2,16,2,200,128]{4,3,2,1,0:T(8,128)S(1)} %bitcast.140), kind=kLoop, calls=%fused_computation.6 | loop fusion | flops 1703936 | bytes 13631488 | tf_op jit(solution)/shard_map/concatenate | solution.py:480
  137.8 53.7 %shard_map.166 = f32[2,8,640]{2,1,0:T(8,128)S(1)} custom-call(f32[2,16,2,208,128]{4,3,2,1,0:T(8,128)} %pad_maximum_fusion.g_ref), custom_call_target="tpu_custom_call" | custom-call | tf_op jit(solution)/shard_map/pallas_call | solution.py:388
  191.5 0.5 slice_bitcast_fusion.2
  192.0 0.6 slice_bitcast_fusion
  (42 shorter events, 0.8 us)
Async XLA Ops:
  0.6 15.2 %copy-start.1 = (bf16[1,1024,1280]{2,1,0:T(8,128)(2,1)S(1)}, bf16[1,1024,1280]{2,1,0:T(8,128)(2,1)}, u32[]{:S(2)}) copy-start(bf16[1,1024,1280]{2,1,0:T(8,128)(2,1)} %param.14) | copy-start | bytes 7864324
  13.2 3.7 %copy-start = (bf16[256,256]{1,0:T(8,128)(2,1)S(1)}, bf16[256,256]{1,0:T(8,128)(2,1)}, u32[]{:S(2)}) copy-start(bf16[256,256]{1,0:T(8,128)(2,1)} %constant.59.clone.sel_ref) | copy-start | bytes 393220
  72.1 3.6 %copy-start.2 = (bf16[1,1024,1280]{2,1,0:T(8,128)(2,1)S(1)}, bf16[1,1024,1280]{2,1,0:T(8,128)(2,1)}, u32[]{:S(2)}) copy-start(bf16[1,1024,1280]{2,1,0:T(8,128)(2,1)} %param.15) | copy-start | bytes 7864324
  75.7 7.8 %copy-start.3 = (f32[1024,640]{0,1:T(8,128)}, f32[1024,640]{0,1:T(8,128)S(1)}, u32[]{:S(2)}) copy-start(f32[1024,640]{0,1:T(8,128)S(1)} %fusion.27) | copy-start | bytes 7864324
  97.8 6.9 %copy-start.4 = (f32[1024,640]{0,1:T(8,128)S(1)}, f32[1024,640]{0,1:T(8,128)}, u32[]{:S(2)}) copy-start(f32[1024,640]{0,1:T(8,128)} %copy-done.3) | copy-start | bytes 7864324
  97.8 6.9 %copy-start.5 = (bf16[1024,1280]{1,0:T(8,128)(2,1)S(1)}, bf16[1024,1280]{1,0:T(8,128)(2,1)}, u32[]{:S(2)}) copy-start(bf16[1024,1280]{1,0:T(8,128)(2,1)} %fusion.24) | copy-start | bytes 7864324

commit v2 on v0

v2 whole, which is shorter than its diff:
```python
import functools
import math

import jax
import jax.numpy as jnp
import numpy as np
from jax import lax
from jax.experimental import pallas as pl
from jax.experimental.pallas import tpu as pltpu
from jax.sharding import PartitionSpec as P

GROUPS = 32
STEPS_T = 1000
EPS = 1e-05
MESH = pl.DeviceIdType.MESH
F32 = jnp.float32
BF16 = jnp.bfloat16


def dev(y, z, x, c):
    return ((y * 8 + z) * 4 + x) * 2 + c


def where_am_i():
    me = lax.axis_index("dp")
    c = lax.rem(me, 2)
    x = lax.rem(lax.div(me, 2), 4)
    z = lax.rem(lax.div(me, 8), 8)
    y = lax.div(me, 64)
    return y, z, x, c


class Ring:
    def __init__(self, b, y, z, x, c):
        r = lax.rem(c + b, 2)
        self.r = r
        self.p = (1 - r) * y + r * x
        self.q = (1 - r) * x + r * y
        self.at = (y, z, x, c)

    def block(self, dp, dq):
        pp = lax.rem(self.p + dp, 4)
        qq = lax.rem(self.q + dq, 4)
        return pp * (4 - 3 * self.r) + qq * (1 + 3 * self.r)

    def first(self, d):
        y, z, x, c = self.at
        r = self.r
        return dev(lax.rem(y + (1 - r) * d, 4), z, lax.rem(x + r * d, 4), c)

    def second(self, d):
        y, z, x, c = self.at
        r = self.r
        return dev(lax.rem(y + r * d, 4), z, lax.rem(x + (1 - r) * d, 4), c)


def signal(device):
    pl.semaphore_signal(pltpu.get_barrier_semaphore(), inc=1, device_id=(device,), device_id_type=MESH)


def remote(src, dst, ssem, rsem, device):
    return pltpu.make_async_remote_copy(
        src_ref=src, dst_ref=dst, send_sem=ssem, recv_sem=rsem, device_id=(device,), device_id_type=MESH
    )


def greet_planes(y, z, x, c):
    for d in (1, 3):
        signal(dev(y, z, lax.rem(x + d, 4), c))
        signal(dev(lax.rem(y + d, 4), z, x, c))
    signal(dev(y, z, x, 1 - c))


ROWS = 256
STEPS = 4


def plan_of(step):
    index = lax.broadcasted_iota(jnp.int32, (8, 128), 0) * 128 + lax.broadcasted_iota(jnp.int32, (8, 128), 1)
    lo = math.sqrt(0.00085)
    hi = math.sqrt(0.012)
    betas = (lo + (hi - lo) * index.astype(F32) / (STEPS_T - 1)) ** 2
    logs = jnp.where(index <= step, jnp.log(1.0 - betas), 0.0)
    return jnp.exp(jnp.sum(jnp.sum(logs, axis=1, keepdims=True), axis=0, keepdims=True))


def embed(tval, width):
    half = width // 2
    lane = lax.broadcasted_iota(jnp.int32, (8, width), 1)
    index = jnp.where(lane < half, lane, lane - half).astype(F32)
    angles = tval * jnp.exp(-math.log(10000.0) * index / half)
    return jnp.where(lane < half, jnp.cos(angles), jnp.sin(angles))


def by_parts(value, indicator, dims):
    total = None
    for _ in range(3):
        part = value.astype(BF16)
        value = value - part.astype(F32)
        term = lax.dot_general(part, indicator, (dims, ((), ())), preferred_element_type=F32)
        total = term if total is None else total + term
    return total


def per_group(sums, indicator, count):
    groups = by_parts(sums, indicator, ((1,), (0,)))
    return jnp.broadcast_to(jnp.sum(groups, axis=0, keepdims=True), groups.shape) / count


def per_channel(groups, indicator):
    return by_parts(groups, indicator, ((1,), (1,)))


def eights(value):
    return jnp.sum(value.reshape(value.shape[0] // 8, 8, value.shape[1]), axis=0)


def kernel(
    feat_hbm, noise_hbm, critic_hbm, s_step, t_step, si_ref, so_ref, ti_ref, to_ref, vecs_ref, sel_ref, ind_ref,
    o_ref,
    feat, noise, critic, rawf, raw, rbuf, wb, w, vec, hid, pre, act, sample, dpre, sums, stat, emb,
    grad, sib, t1, fm, fp, acc, u1, um, up, stage, fin,
    l_sem, r_send, r_recv, s_send, s_recv, s_sib,
    h_send, h_recv, q_send, t_recv, m_recv, p_recv, p_send, ut_recv, um_recv, up_recv, f_send, f_recv,
):
    y, z, x, c = where_am_i()
    mine = lax.div(z, 2) == x
    selfish = (2 * x + c) == z
    loads = [
        pltpu.make_async_copy(src.at[0], dst, l_sem.at[n])
        for n, (src, dst) in enumerate(((feat_hbm, feat), (noise_hbm, noise), (critic_hbm, critic)))
    ]
    loads[0].start()

    greet_planes(y, z, x, c)
    for k in range(1, 16):
        signal(dev(y, 2 * x + lax.rem(z + k // 8, 2), lax.rem(x + k // 2, 4), lax.rem(c + k, 2)))

    @pl.when(jnp.logical_not(mine))
    def _():
        signal(dev(y, 2 * x + lax.rem(z, 2), x, c))

    for k in range(1, 8):
        signal(dev(y, lax.rem(z + k, 8), lax.div(z, 2), lax.rem(z, 2)))

    @pl.when(jnp.logical_not(selfish))
    def _():
        signal(dev(y, z, lax.div(z, 2), lax.rem(z, 2)))

    rawf[...] = jnp.zeros_like(rawf)
    place = 5 * lax.rem(lax.axis_index("dp"), 16)
    spread = pltpu.roll(vecs_ref[...], place, 1)
    for core, pair in enumerate(((si_ref, ti_ref), (so_ref, to_ref))):
        for b, ref in enumerate(pair):
            shard = ref[...].astype(F32)
            for j in range(5):
                r = 16 * (2 * b + j // 3) + 5 * (j % 3)
                rawf[core, r : r + 5, :] = shard[:, 128 * j : 128 * j + 128]
            for h in range(2):
                r = 16 * (2 * b + h) + 15
                rawf[core, r : r + 1, :] = spread[2 * b + h : 2 * b + h + 1]
    raw[...] = rawf[...].astype(BF16)
    loads[0].wait()
    loads[1].start()
    loads[2].start()

    def rows_of(i):
        return pl.ds(pl.multiple_of(i * ROWS, ROWS), ROWS)

    sums[...] = jnp.zeros_like(sums)

    @pl.loop(0, STEPS)
    def _(i):
        sums[0] += eights(feat[rows_of(i), :].astype(F32))

    pl.semaphore_wait(pltpu.get_barrier_semaphore(), jnp.where(mine, 20, 21) + jnp.where(selfish, 7, 8))

    slot = lax.rem(z, 2) * 8 + x * 2 + c
    to_x = lax.div(z, 2)
    own = pltpu.make_async_copy(raw.at[c], rbuf.at[slot], r_recv)
    for k in range(1, 16):
        cc = lax.rem(c + k, 2)
        remote(raw.at[cc], rbuf.at[slot], r_send, r_recv, dev(y, lax.rem(z + k // 2, 8), to_x, cc)).start()
    first = remote(raw.at[c], rbuf.at[slot], r_send, r_recv, dev(y, z, to_x, c))

    @pl.when(mine)
    def _():
        own.start()

    @pl.when(jnp.logical_not(mine))
    def _():
        first.start()

    count = 40 * 1024

    def mean_to(b):
        stat[b, 0:8, :] = per_channel(per_group(sums[0], ind_ref[...], count), ind_ref[...])

    def scale_to(b):
        var = per_group(sums[1], ind_ref[...], count)
        stat[b, 8:16, :] = per_channel(lax.rsqrt(var + EPS), ind_ref[...])

    mean_to(0)

    @pl.loop(0, STEPS)
    def _(i):
        off = feat[rows_of(i), :].astype(F32) - stat[0, 0:1, :]
        sums[1] += eights(off * off)

    scale_to(0)
    emb[0] = embed((999 - 250 * s_step[0]).astype(F32), 640)
    emb[1] = embed(t_step[0].astype(F32), 640)

    rings = [Ring(b, y, z, x, c) for b in range(2)]

    def at(b, g):
        return wb.at[(b * 2 + c) * 16 + g]

    def send(b, g, device):
        remote(at(b, g), at(b, g), s_send.at[b], s_recv.at[b, g], device).start()

    def hand(b, g):
        remote(at(b, g), at(b, g), s_send.at[b], s_sib.at[b], dev(y, z, x, 1 - c)).start()

    def wait(b, g):
        remote(at(b, g), at(b, g), s_send.at[b], s_recv.at[b, g], dev(y, z, x, 1 - c)).wait_recv()

    pltpu.make_async_copy(rbuf, rbuf, r_recv).wait()
    row = lax.broadcasted_iota(jnp.int32, (16, 128), 0)
    for b in range(2):
        ring = rings[b]
        g = ring.block(0, 0)
        k = (b * 2 + c) * 16 + g
        outs = []
        for h in range(2):
            t = 2 * b + h
            tile = rbuf[:, 16 * t : 16 * t + 16, :].reshape(256, 128)
            out = jnp.dot(sel_ref[...], tile, preferred_element_type=F32)
            outs.append(out[240:256])
            for i in range(3):
                j = 3 * h + i
                if j < 5:
                    wb[k, 80 * j : 80 * j + 80, :] = out[80 * i : 80 * i + 80].astype(BF16)
        wb[k, 400:416, :] = jnp.where(row == 0, outs[0], outs[1]).astype(BF16)
        send(b, g, ring.first(1))
        send(b, g, ring.first(3))
        send(b, g, ring.second(1))
        send(b, g, ring.second(3))
        hand(b, g)

    def gather_first(b):
        ring = rings[b]
        for d in (3, 1, 2):
            g = ring.block(d, 0)
            wait(b, g)
            if d == (3 if b == 0 else 1):
                send(b, g, ring.first(1 if b == 0 else 3))
            send(b, g, ring.second(1))
            send(b, g, ring.second(3))
            hand(b, g)

    def gather_second(b, n):
        ring = rings[b]
        d = (0, 3, 1, 2)[n]
        for e in (3, 1):
            g = ring.block(d, e)
            wait(b, g)
            if e == (3 if n % 2 == 0 else 1):
                send(b, g, ring.second(1 if e == 3 else 3))
            hand(b, g)

    def gather_last(b):
        for d in (0, 3, 1, 2):
            g = rings[b].block(d, 2)
            wait(b, g)
            hand(b, g)

    def gathered(b):
        pltpu.make_async_copy(wb.at[pl.ds(0, 16)], wb.at[pl.ds(0, 16)], s_sib.at[b]).wait()
        for n in (2 * b, 2 * b + 1):
            for j in range(5):
                w[n, :, 128 * j : 128 * j + 128] = wb[16 * n : 16 * n + 16, 80 * j : 80 * j + 80, :].reshape(1280, 128)
        lane = lax.broadcasted_iota(jnp.int32, (16, 128), 1)
        parts = [jnp.zeros((16, 128), F32) for _ in range(10)]
        for g in range(16):
            tile, s = divmod(80 * g, 128)
            v = wb[2 * b * 16 + g, 400:416, :].astype(F32)
            if s:
                v = pltpu.roll(v, s, 1)
            parts[tile] += jnp.where(lane >= s, v, 0.0)
            if s + 80 > 128:
                parts[tile + 1] += jnp.where(lane < s, v, 0.0)
        for n in range(10):
            vec[b, :, 128 * n : 128 * n + 128] = parts[n]

    gather_first(0)
    gather_first(1)
    for n in range(4):
        gather_second(0, n)
    gather_last(0)
    gathered(0)

    keep = plan_of(t_step[0])
    root, other_root = jnp.sqrt(keep), jnp.sqrt(1.0 - keep)
    nt = (((1,), (1,)), ((), ()))
    sums[...] = jnp.zeros_like(sums)
    loads[1].wait()

    @pl.loop(0, STEPS)
    def _(i):
        s = rows_of(i)
        field = feat[s, :].astype(F32)
        normed = (field - stat[0, 0:1, :]) * stat[0, 8:9, :]
        hid[s, :] = (normed * vec[0, 0:1, :] + vec[0, 1:2, :]).astype(BF16)
        u = jnp.dot(hid[s, :], w[0], preferred_element_type=F32) + emb[0, 0:1, :]
        pre[s, :] = u
        act[s, :] = (u * jax.nn.sigmoid(u)).astype(BF16)
        out = field + lax.dot_general(act[s, :], w[1], nt, preferred_element_type=F32)
        sample[s, :] = out
        noisy = (root * out + other_root * noise[s, :].astype(F32)).astype(BF16)
        noise[s, :] = noisy
        sums[0] += eights(noisy.astype(F32))
        for n in range(4):

            @pl.when(i == n)
            def _(n=n):
                gather_second(1, n)

    gather_last(1)
    mean_to(1)

    @pl.loop(0, STEPS)
    def _(i):
        off = noise[rows_of(i), :].astype(F32) - stat[1, 0:1, :]
        sums[1] += eights(off * off)

    scale_to(1)
    gathered(1)
    loads[2].wait()

    norm = 1.0 / 512.0

    @pl.loop(0, STEPS)
    def _(i):
        s = rows_of(i)
        field = noise[s, :].astype(F32)
        normed = (field - stat[1, 0:1, :]) * stat[1, 8:9, :]
        h = (normed * vec[1, 0:1, :] + vec[1, 1:2, :]).astype(BF16)
        u = jnp.dot(h, w[2], preferred_element_type=F32) + emb[1, 0:1, :]
        a = (u * jax.nn.sigmoid(u)).astype(BF16)
        target = field + lax.dot_general(a, w[3], nt, preferred_element_type=F32)
        critic[s, :] = ((2.0 * keep * (sample[s, :] - target) + critic[s, :].astype(F32)) * norm).astype(BF16)

    def to_sibling(b, g):
        return remote(grad.at[b, g, 1 - c], sib.at[b, g], h_send.at[b], h_recv.at[b, g], dev(y, z, x, 1 - c))

    def term(b, left, right):
        for tile in range(2):
            out = lax.dot_general(
                left[:, 640 * tile : 640 * tile + 640], right[...], (((0,), (0,)), ((), ())), preferred_element_type=F32
            )
            for n in range(8):
                for h in range(2):
                    for j in range(5):
                        grad[b, 8 * tile + n, h, 40 * j : 40 * j + 40, :] = out[
                            80 * n + 40 * h : 80 * n + 40 * h + 40, 128 * j : 128 * j + 128
                        ]
            for n in range(8):
                to_sibling(b, 8 * tile + n).start()

    for g in range(16):
        for h in range(2):
            grad[0, g, h, 200:208, :] = jnp.zeros((8, 128), F32)
    term(0, critic, act)

    def meet(b, g):
        to_sibling(b, g).wait_recv()
        sib[b, g] += grad[b, g, c]

    def push(b, g, dst, recv, d):
        remote(sib.at[b, g], dst, q_send.at[b], recv, rings[b].second(d)).start()

    def reduce_far(b):
        for k in range(4):
            g = rings[b].block((2, 1, 3, 0)[k], 2)
            meet(b, g)
            push(b, g, t1.at[b, k], t_recv.at[b, k], 1 if k % 2 == 0 else 3)

    def reduce_near(b, k):
        d = (2, 1, 3, 0)[k]
        for e in (3, 1) if k % 2 == 0 else (1, 3):
            g = rings[b].block(d, e)
            meet(b, g)
            if e == (1 if k % 2 == 0 else 3):
                remote(t1.at[b, k], t1.at[b, k], q_send.at[b], t_recv.at[b, k], rings[b].second(1)).wait_recv()
                sib[b, g] += t1[b, k]
            if e == 1:
                push(b, g, fm.at[b, k], m_recv.at[b, k], 1)
            else:
                push(b, g, fp.at[b, k], p_recv.at[b, k], 3)

    def arrive(b, dst, recv):
        remote(dst, dst, p_send.at[b], recv, rings[b].first(1)).wait_recv()

    def reduce_first(b, k):
        ring = rings[b]

        def push1(dst, recv, d):
            remote(acc.at[b, k], dst, p_send.at[b], recv, ring.first(d)).start()

        d = (2, 1, 3, 0)[k] if b == 0 else (2, 3, 1, 0)[k]
        kk = (2, 1, 3, 0).index(d)
        g = ring.block(d, 0)
        meet(b, g)
        arrive(b, fm.at[b, kk], m_recv.at[b, kk])
        arrive(b, fp.at[b, kk], p_recv.at[b, kk])
        acc[b, k] = sib[b, g] + fm[b, kk] + fp[b, kk]
        if k == 0:
            push1(u1.at[b], ut_recv.at[b], 1 if b == 0 else 3)
        if k == 1:
            arrive(b, u1.at[b], ut_recv.at[b])
            acc[b, k] += u1[b]
        if k in (1, 2):
            if d == 1:
                push1(um.at[b], um_recv.at[b], 1)
            else:
                push1(up.at[b], up_recv.at[b], 3)

    def pieces(b):
        arrive(b, um.at[b], um_recv.at[b])
        arrive(b, up.at[b], up_recv.at[b])
        total = acc[b, 3] + um[b] + up[b]
        for s in range(8):
            for j in range(5):
                stage[b, s, 0:5, 128 * j : 128 * j + 128] = total[40 * j + 5 * s : 40 * j + 5 * s + 5]
            v = total[200:208]
            if s:
                v = pltpu.roll(v, 128 - 5 * s, 1)
            stage[b, s, 5:7, 0:128] = v[0:2]
        for k in range(1, 8):
            s = lax.rem(x * 2 + c + k, 8)
            remote(
                stage.at[b, s], fin.at[b, z], f_send.at[b], f_recv.at[b],
                dev(y, 2 * x + c, lax.div(s, 2), lax.rem(s, 2)),
            ).start()
        s = x * 2 + c
        stay = pltpu.make_async_copy(stage.at[b, s], fin.at[b, z], f_recv.at[b])
        go = remote(stage.at[b, s], fin.at[b, z], f_send.at[b], f_recv.at[b], dev(y, 2 * x + c, x, c))

        @pl.when(selfish)
        def _():
            stay.start()

        @pl.when(jnp.logical_not(selfish))
        def _():
            go.start()

    sums[...] = jnp.zeros_like(sums)

    @pl.loop(0, STEPS)
    def _(i):
        s = rows_of(i)
        d_act = jnp.dot(critic[s, :], w[1], preferred_element_type=F32)
        u = pre[s, :]
        sig = jax.nn.sigmoid(u)
        dp = (d_act * sig * (1.0 + u * (1.0 - sig))).astype(BF16)
        dpre[s, :] = dp
        d_hid = lax.dot_general(dp, w[0], nt, preferred_element_type=F32)
        normed = (feat[s, :].astype(F32) - stat[0, 0:1, :]) * stat[0, 8:9, :]
        sums[0] += eights(d_hid * normed)
        sums[1] += eights(d_hid)

        @pl.when(i == 0)
        def _():
            reduce_far(0)

        @pl.when(i == 2)
        def _():
            reduce_near(0, 0)
            reduce_near(0, 1)

        @pl.when(i == 3)
        def _():
            reduce_near(0, 2)
            reduce_near(0, 3)

    top = lax.broadcasted_iota(jnp.int32, (8, 128), 0) == 0
    lane8 = lax.broadcasted_iota(jnp.int32, (8, 128), 1)
    lines = []
    for n in range(10):
        gains = jnp.sum(sums[0, :, 128 * n : 128 * n + 128], axis=0, keepdims=True)
        shifts = jnp.sum(sums[1, :, 128 * n : 128 * n + 128], axis=0, keepdims=True)
        lines.append(jnp.where(top, gains, shifts))
    for n in range(32):
        tile, s = divmod(40 * n, 128)
        v = pltpu.roll(lines[tile], 128 - s, 1) if s else lines[tile]
        if s + 40 > 128:
            v = jnp.where(lane8 < 128 - s, v, pltpu.roll(lines[tile + 1], 128 - s, 1))
        grad[1, n // 2, n % 2, 200:208, :] = v
    term(1, hid, dpre)

    for k in range(4):
        reduce_first(0, k)
    reduce_far(1)
    pieces(0)
    for k in range(4):
        reduce_near(1, k)
    for k in range(4):
        reduce_first(1, k)
    pieces(1)

    for b in range(2):
        pltpu.make_async_copy(fin.at[b], fin.at[b], f_recv.at[b]).wait()
        o_ref[b] = jnp.sum(fin[b], axis=0)

    @pl.when(mine)
    def _():
        pltpu.make_async_copy(rbuf.at[pl.ds(0, 15)], rbuf.at[pl.ds(0, 15)], r_send).wait()

    @pl.when(jnp.logical_not(mine))
    def _():
        pltpu.make_async_copy(rbuf, rbuf, r_send).wait()

    for b in range(2):
        pltpu.make_async_copy(wb.at[pl.ds(0, 31)], wb.at[pl.ds(0, 31)], s_send.at[b]).wait()
        pltpu.make_async_copy(sib.at[b], sib.at[b], h_send.at[b]).wait()
        pltpu.make_async_copy(sib.at[b, pl.ds(0, 12)], sib.at[b, pl.ds(0, 12)], q_send.at[b]).wait()
        pltpu.make_async_copy(acc.at[b, pl.ds(0, 3)], acc.at[b, pl.ds(0, 3)], p_send.at[b]).wait()

        @pl.when(selfish)
        def _():
            pltpu.make_async_copy(fin.at[b, pl.ds(0, 7)], fin.at[b, pl.ds(0, 7)], f_send.at[b]).wait()

        @pl.when(jnp.logical_not(selfish))
        def _():
            pltpu.make_async_copy(fin.at[b], fin.at[b], f_send.at[b]).wait()


def selection():
    sel = np.zeros((256, 256), np.float32)
    for m in range(240):
        i, q = divmod(m, 80)
        sel[m, 16 * (q // 5) + 5 * i + q % 5] = 1.0
    for d in range(16):
        sel[240:242, 16 * d + 15] = 1.0
    return jnp.asarray(sel, BF16)


def membership():
    ind = np.zeros((1280, 128), np.float32)
    ind[np.arange(1280), np.arange(1280) // 40] = 1.0
    return jnp.asarray(ind, BF16)


def local(
    features,
    renoise,
    critic_grad,
    student_step,
    teacher_step,
    student_in,
    student_gain,
    student_shift,
    student_out,
    teacher_in,
    teacher_gain,
    teacher_shift,
    teacher_out,
):
    vecs = jnp.stack([student_gain, student_shift, teacher_gain, teacher_shift]).astype(F32)
    vecs = jnp.pad(vecs, ((0, 4), (0, 123)))
    vmem = pl.BlockSpec(memory_space=pltpu.VMEM)
    smem = pl.BlockSpec(memory_space=pltpu.SMEM)
    hbm = pl.BlockSpec(memory_space=pl.ANY)
    half = (208, 128)
    dma = pltpu.SemaphoreType.DMA
    out = pl.pallas_call(
        kernel,
        out_shape=jax.ShapeDtypeStruct((2, 8, 640), F32),
        in_specs=[hbm] * 3 + [smem] * 2 + [vmem] * 7,
        out_specs=vmem,
        scratch_shapes=[
            pltpu.VMEM((1024, 1280), BF16),
            pltpu.VMEM((1024, 1280), BF16),
            pltpu.VMEM((1024, 1280), BF16),
            pltpu.VMEM((2, 64, 128), F32),
            pltpu.VMEM((2, 64, 128), BF16),
            pltpu.VMEM((16, 64, 128), BF16),
            pltpu.VMEM((64, 416, 128), BF16),
            pltpu.VMEM((4, 1280, 640), BF16),
            pltpu.VMEM((2, 16, 1280), F32),
            pltpu.VMEM((1024, 1280), BF16),
            pltpu.VMEM((1024, 640), F32),
            pltpu.VMEM((1024, 640), BF16),
            pltpu.VMEM((1024, 1280), F32),
            pltpu.VMEM((1024, 640), BF16),
            pltpu.VMEM((2, 8, 1280), F32),
            pltpu.VMEM((2, 16, 1280), F32),
            pltpu.VMEM((2, 8, 640), F32),
            pltpu.VMEM((2, 16, 2, *half), F32),
            pltpu.VMEM((2, 16, *half), F32),
            pltpu.VMEM((2, 4, *half), F32),
            pltpu.VMEM((2, 4, *half), F32),
            pltpu.VMEM((2, 4, *half), F32),
            pltpu.VMEM((2, 4, *half), F32),
            pltpu.VMEM((2, *half), F32),
            pltpu.VMEM((2, *half), F32),
            pltpu.VMEM((2, *half), F32),
            pltpu.VMEM((2, 8, 8, 640), F32),
            pltpu.VMEM((2, 8, 8, 640), F32),
            dma((3,)),
            dma,
            dma,
            dma((2,)),
            dma((2, 16)),
            dma((2,)),
            dma((2,)),
            dma((2, 16)),
            dma((2,)),
            dma((2, 4)),
            dma((2, 4)),
            dma((2, 4)),
            dma((2,)),
            dma((2,)),
            dma((2,)),
            dma((2,)),
            dma((2,)),
            dma((2,)),
        ],
        compiler_params=pltpu.CompilerParams(collective_id=0, has_side_effects=True, vmem_limit_bytes=62 * 2**20),
    )(
        features, renoise, critic_grad, student_step, teacher_step, student_in, student_out.T, teacher_in, teacher_out.T,
        vecs, selection(), membership(),
    )
    return out[1, :5], out[0, :5].T, out[1, 5, :5], out[1, 6, :5]


def solution(mesh):
    return jax.shard_map(
        local,
        mesh=mesh,
        in_specs=(
            P("dp", None, None),
            P("dp", None, None),
            P("dp", None, None),
            P("dp"),
            P("dp"),
            P("dp", None),
            P("dp"),
            P("dp"),
            P(None, "dp"),
            P("dp", None),
            P("dp"),
            P("dp"),
            P(None, "dp"),
        ),
        out_specs=(P("dp", None), P(None, "dp"), P("dp"), P("dp")),
        check_vma=False,
    )
```

time: 756 us -> 117 us (0.15)
  waiting for transfers between devices: 510 us -> 0 us
  blocking collectives: 160 us -> 0 us
  Pallas kernels: 0 us -> 110 us
  matrix products: 37.9 us -> 0 us
  local copies, waits for them, and re-layouts: 22.5 us -> 2.64 us
  between operations: 17.4 us -> 1.93 us
    all_gather x4 -> x0, waiting for transfers between devices: 317 us -> none  [the longest x1 104 us: local(): lax.all_gather(student_out, 'dp', axis=1, tiled=True)]
    unnamed x6 -> x0, waiting for transfers between devices: 192 us -> none
    unnamed x2 -> x0, blocking collectives: 160 us -> none
    pallas_call x0 -> x1, Pallas kernels: none -> 110 us  [local(): pl.pallas_call(kernel, out_shape=jax.ShapeDtypeStruct((2, 8, 640), F32),...]
    dot_general x7 -> x0, matrix products: 37.9 us -> none  [the longest x2 15.8 us: block(): jnp.dot(act.reshape(batch * rows, -1), w_out, preferred_element_type=jnp....]
    unnamed x37 -> x0, local copies, waits for them, and re-layouts: 20 us -> none
  transfers between devices with their start and end apart: 5 -> 0, of which waited for: 5 -> 0; matrix products, arithmetic and copies ran while one was open for 5% -> 0% of each run, Pallas kernels for 0% -> 0%
where the time goes in v2:
time: 117 us; the launch traced here: 115 us
  Pallas kernels  110 us (94%)
  local copies, waits for them, and re-layouts  2.64 us (2%)
  between operations  1.93 us (2%)
  other arithmetic  1.31 us (1%)
    pallas_call x1, Pallas kernels, local(): pl.pallas_call(kernel, out_shape=jax.ShapeDtypeStruct((2, 8, 640), F32),...  110 us

profile of v2, /device:TPU:1, one launch (start us, length us, event | category | flops | bytes accessed | tf_op | source)
XLA Modules:
  0.0 115.4 jit_solution(5795686148658481634)
XLA Ops:
  1.9 1.3 %fusion.9.vecs_ref = f32[8,128]{1,0:T(8,128)} fusion(bf16[1,5]{1,0:T(2,128)(2,1)} %bitcast.18, bf16[1,5]{1,0:T(2,128)(2,1)} %bitcast.19, bf16[1,5]{1,0:T(2,128)(2,1)} %bitcast.20, bf16[1,5]{1,0:T(2,128)(2,1)} %bitcast.21), kind=kLoop, calls=%fused_computation.13 | loop fusion | flops 19456 | bytes 4136 | tf_op jit(solution)/shard_map/jit(_pad)/pad | solution.py:571
  3.2 109.5 %shard_map.174 = f32[2,8,640]{2,1,0:T(8,128)} custom-call(bf16[1,1024,1280]{2,1,0:T(8,128)(2,1)} %feat_hbm.1, bf16[1,1024,1280]{2,1,0:T(8,128)(2,1)} %noise_hbm.1, bf16[1,1024,1280]{2,1,0:T(8,128)(2,1)} %critic_hbm.1, s32[1]{0:T(128)S(6)} %copy.19.s_step, s32[1]{0:T(128)S(6)} %copy.20.t_step, bf16[5,640]{1,0:T(8,128)(2,1)} %si_ref.1, ...), custom_call_target="tpu_custom_call" | custom-call | tf_op jit(solution)/shard_map/pallas_call | solution.py:577
  112.8 1.3 %slice_bitcast_fusion.2 = (f32[5]{0:T(128)}, f32[5]{0:T(128)}) fusion(f32[2,8,640]{2,1,0:T(8,128)} %shard_map.174), kind=kLoop, calls=%fused_computation.17 | loop fusion | bytes 80 | tf_op jit(solution)/shard_map/squeeze | solution.py:635
  114.1 1.4 %slice_bitcast_fusion = (f32[640,5]{0,1:T(8,128)}, f32[5,640]{1,0:T(8,128)}) fusion(f32[2,8,640]{2,1,0:T(8,128)} %shard_map.174), kind=kLoop, calls=%fused_computation | loop fusion | bytes 51200 | tf_op jit(solution)/shard_map/transpose | solution.py:635

commit v3 on v2

--- a/solution.py
+++ b/solution.py
@@ -65,7 +65,7 @@
 
 
 def greet_planes(y, z, x, c):
-    for d in (1, 3):
+    for d in (1, 2, 3):
         signal(dev(y, z, lax.rem(x + d, 4), c))
         signal(dev(lax.rem(y + d, 4), z, x, c))
     signal(dev(y, z, x, 1 - c))
@@ -116,16 +116,15 @@
 
 
 def kernel(
-    feat_hbm, noise_hbm, critic_hbm, s_step, t_step, si_ref, so_ref, ti_ref, to_ref, vecs_ref, sel_ref, ind_ref,
-    o_ref,
-    feat, noise, critic, rawf, raw, rbuf, wb, w, vec, hid, pre, act, sample, dpre, sums, stat, emb,
-    grad, sib, t1, fm, fp, acc, u1, um, up, stage, fin,
+    feat_hbm, noise_hbm, critic_hbm, s_step, t_step, si_ref, so_ref, ti_ref, to_ref, sg_ref, ss_ref, tg_ref, ts_ref, sel_ref, ind_ref,
+    in_ref, out_ref, gain_ref, shift_ref,
+    feat, noise, critic, vecs, rawf, raw, rbuf, wb, w, vec, hid, pre, act, sample, dpre, sums, stat, emb,
+    grad, sib, t1, fm, fp, acc, u1, um, up, stage, mid, fin,
     l_sem, r_send, r_recv, s_send, s_recv, s_sib,
-    h_send, h_recv, q_send, t_recv, m_recv, p_recv, p_send, ut_recv, um_recv, up_recv, f_send, f_recv,
+    h_send, h_recv, q_send, t_recv, m_recv, p_recv, p_send, ut_recv, um_recv, up_recv, e_send, e_recv, f_send, f_recv,
 ):
     y, z, x, c = where_am_i()
     mine = lax.div(z, 2) == x
-    selfish = (2 * x + c) == z
     loads = [
         pltpu.make_async_copy(src.at[0], dst, l_sem.at[n])
         for n, (src, dst) in enumerate(((feat_hbm, feat), (noise_hbm, noise), (critic_hbm, critic)))
@@ -140,16 +139,17 @@
     def _():
         signal(dev(y, 2 * x + lax.rem(z, 2), x, c))
 
+    for d in (1, 2, 3):
+        signal(dev(y, z, lax.rem(x + d, 4), 1 - c))
     for k in range(1, 8):
-        signal(dev(y, lax.rem(z + k, 8), lax.div(z, 2), lax.rem(z, 2)))
-
-    @pl.when(jnp.logical_not(selfish))
-    def _():
-        signal(dev(y, z, lax.div(z, 2), lax.rem(z, 2)))
+        signal(dev(y, lax.rem(z + k, 8), x, c))
 
     rawf[...] = jnp.zeros_like(rawf)
     place = 5 * lax.rem(lax.axis_index("dp"), 16)
-    spread = pltpu.roll(vecs_ref[...], place, 1)
+    vecs[...] = jnp.zeros_like(vecs)
+    for n, ref in enumerate((sg_ref, ss_ref, tg_ref, ts_ref)):
+        vecs[n : n + 1, 0:5] = ref[...].astype(F32)
+    spread = pltpu.roll(vecs[...], place, 1)
     for core, pair in enumerate(((si_ref, ti_ref), (so_ref, to_ref))):
         for b, ref in enumerate(pair):
             shard = ref[...].astype(F32)
@@ -173,23 +173,30 @@
     def _(i):
         sums[0] += eights(feat[rows_of(i), :].astype(F32))
 
-    pl.semaphore_wait(pltpu.get_barrier_semaphore(), jnp.where(mine, 20, 21) + jnp.where(selfish, 7, 8))
+    pl.semaphore_wait(pltpu.get_barrier_semaphore(), jnp.where(mine, 32, 33))
 
     slot = lax.rem(z, 2) * 8 + x * 2 + c
     to_x = lax.div(z, 2)
-    own = pltpu.make_async_copy(raw.at[c], rbuf.at[slot], r_recv)
-    for k in range(1, 16):
-        cc = lax.rem(c + k, 2)
-        remote(raw.at[cc], rbuf.at[slot], r_send, r_recv, dev(y, lax.rem(z + k // 2, 8), to_x, cc)).start()
-    first = remote(raw.at[c], rbuf.at[slot], r_send, r_recv, dev(y, z, to_x, c))
-
-    @pl.when(mine)
-    def _():
-        own.start()
-
-    @pl.when(jnp.logical_not(mine))
-    def _():
-        first.start()
+    for b in range(2):
+
+        def shard(cc):
+            return raw.at[cc, pl.ds(32 * b, 32)]
+
+        for k in range(1, 16):
+            cc = lax.rem(c + k, 2)
+            remote(
+                shard(cc), rbuf.at[b, slot], r_send.at[b], r_recv.at[b], dev(y, lax.rem(z + k // 2, 8), to_x, cc)
+            ).start()
+        own = pltpu.make_async_copy(shard(c), rbuf.at[b, slot], r_recv.at[b])
+        first = remote(shard(c), rbuf.at[b, slot], r_send.at[b], r_recv.at[b], dev(y, z, to_x, c))
+
+        @pl.when(mine)
+        def _():
+            own.start()
+
+        @pl.when(jnp.logical_not(mine))
+        def _():
+            first.start()
 
     count = 40 * 1024
 
@@ -225,16 +232,15 @@
     def wait(b, g):
         remote(at(b, g), at(b, g), s_send.at[b], s_recv.at[b, g], dev(y, z, x, 1 - c)).wait_recv()
 
-    pltpu.make_async_copy(rbuf, rbuf, r_recv).wait()
     row = lax.broadcasted_iota(jnp.int32, (16, 128), 0)
     for b in range(2):
         ring = rings[b]
         g = ring.block(0, 0)
         k = (b * 2 + c) * 16 + g
+        pltpu.make_async_copy(rbuf.at[b], rbuf.at[b], r_recv.at[b]).wait()
         outs = []
         for h in range(2):
-            t = 2 * b + h
-            tile = rbuf[:, 16 * t : 16 * t + 16, :].reshape(256, 128)
+            tile = rbuf[b, :, 16 * h : 16 * h + 16, :].reshape(256, 128)
             out = jnp.dot(sel_ref[...], tile, preferred_element_type=F32)
             outs.append(out[240:256])
             for i in range(3):
@@ -244,6 +250,7 @@
         wb[k, 400:416, :] = jnp.where(row == 0, outs[0], outs[1]).astype(BF16)
         send(b, g, ring.first(1))
         send(b, g, ring.first(3))
+        send(b, g, ring.first(2))
         send(b, g, ring.second(1))
         send(b, g, ring.second(3))
         hand(b, g)
@@ -253,21 +260,17 @@
         for d in (3, 1, 2):
             g = ring.block(d, 0)
             wait(b, g)
-            if d == (3 if b == 0 else 1):
-                send(b, g, ring.first(1 if b == 0 else 3))
             send(b, g, ring.second(1))
             send(b, g, ring.second(3))
             hand(b, g)
 
-    def gather_second(b, n):
+    def gather_second(b, n, e):
         ring = rings[b]
-        d = (0, 3, 1, 2)[n]
-        for e in (3, 1):
-            g = ring.block(d, e)
-            wait(b, g)
-            if e == (3 if n % 2 == 0 else 1):
-                send(b, g, ring.second(1 if e == 3 else 3))
-            hand(b, g)
+        g = ring.block((0, 3, 1, 2)[n], e)
+        wait(b, g)
+        if e == (3 if n % 2 == 0 else 1):
+            send(b, g, ring.second(1 if e == 3 else 3))
+        hand(b, g)
 
     def gather_last(b):
         for d in (0, 3, 1, 2):
@@ -296,7 +299,8 @@
     gather_first(0)
     gather_first(1)
     for n in range(4):
-        gather_second(0, n)
+        gather_second(0, n, 3)
+        gather_second(0, n, 1)
     gather_last(0)
     gathered(0)
 
@@ -315,6 +319,12 @@
         u = jnp.dot(hid[s, :], w[0], preferred_element_type=F32) + emb[0, 0:1, :]
         pre[s, :] = u
         act[s, :] = (u * jax.nn.sigmoid(u)).astype(BF16)
+        for n in range(4):
+
+            @pl.when(i == n)
+            def _(n=n):
+                gather_second(1, n, 3)
+
         out = field + lax.dot_general(act[s, :], w[1], nt, preferred_element_type=F32)
         sample[s, :] = out
         noisy = (root * out + other_root * noise[s, :].astype(F32)).astype(BF16)
@@ -324,7 +334,7 @@
 
             @pl.when(i == n)
             def _(n=n):
-                gather_second(1, n)
+                gather_second(1, n, 1)
 
     gather_last(1)
     mean_to(1)
@@ -373,9 +383,12 @@
             grad[0, g, h, 200:208, :] = jnp.zeros((8, 128), F32)
     term(0, critic, act)
 
-    def meet(b, g):
+    def meet(b, g, *more):
         to_sibling(b, g).wait_recv()
-        sib[b, g] += grad[b, g, c]
+        total = sib[b, g] + grad[b, g, c]
+        for ref in more:
+            total += ref[...]
+        return total
 
     def push(b, g, dst, recv, d):
         remote(sib.at[b, g], dst, q_send.at[b], recv, rings[b].second(d)).start()
@@ -383,53 +396,48 @@
     def reduce_far(b):
         for k in range(4):
             g = rings[b].block((2, 1, 3, 0)[k], 2)
-            meet(b, g)
+            sib[b, g] = meet(b, g)
             push(b, g, t1.at[b, k], t_recv.at[b, k], 1 if k % 2 == 0 else 3)
 
-    def reduce_near(b, k):
-        d = (2, 1, 3, 0)[k]
-        for e in (3, 1) if k % 2 == 0 else (1, 3):
-            g = rings[b].block(d, e)
-            meet(b, g)
-            if e == (1 if k % 2 == 0 else 3):
-                remote(t1.at[b, k], t1.at[b, k], q_send.at[b], t_recv.at[b, k], rings[b].second(1)).wait_recv()
-                sib[b, g] += t1[b, k]
+    def reduce_direct(b):
+        for k in range(4):
+            e = 3 if k % 2 == 0 else 1
+            g = rings[b].block((2, 1, 3, 0)[k], e)
+            sib[b, g] = meet(b, g)
             if e == 1:
                 push(b, g, fm.at[b, k], m_recv.at[b, k], 1)
             else:
                 push(b, g, fp.at[b, k], p_recv.at[b, k], 3)
 
+    def reduce_through(b):
+        for k in range(4):
+            e = 1 if k % 2 == 0 else 3
+            g = rings[b].block((2, 1, 3, 0)[k], e)
+            remote(t1.at[b, k], t1.at[b, k], q_send.at[b], t_recv.at[b, k], rings[b].second(1)).wait_recv()
+            sib[b, g] = meet(b, g, t1.at[b, k])
+            if e == 1:
+                push(b, g, fm.at[b, k], m_recv.at[b, k], 1)
+            else:
+                push(b, g, fp.at[b, k], p_recv.at[b, k], 3)
+
     def arrive(b, dst, recv):
         remote(dst, dst, p_send.at[b], recv, rings[b].first(1)).wait_recv()
 
     def reduce_first(b, k):
-        ring = rings[b]
-
-        def push1(dst, recv, d):
-            remote(acc.at[b, k], dst, p_send.at[b], recv, ring.first(d)).start()
-
-        d = (2, 1, 3, 0)[k] if b == 0 else (2, 3, 1, 0)[k]
-        kk = (2, 1, 3, 0).index(d)
-        g = ring.block(d, 0)
-        meet(b, g)
-        arrive(b, fm.at[b, kk], m_recv.at[b, kk])
-        arrive(b, fp.at[b, kk], p_recv.at[b, kk])
-        acc[b, k] = sib[b, g] + fm[b, kk] + fp[b, kk]
-        if k == 0:
-            push1(u1.at[b], ut_recv.at[b], 1 if b == 0 else 3)
-        if k == 1:
-            arrive(b, u1.at[b], ut_recv.at[b])
-            acc[b, k] += u1[b]
-        if k in (1, 2):
-            if d == 1:
-                push1(um.at[b], um_recv.at[b], 1)
-            else:
-                push1(up.at[b], up_recv.at[b], 3)
+        g = rings[b].block((2, 1, 3, 0)[k], 0)
+        arrive(b, fm.at[b, k], m_recv.at[b, k])
+        arrive(b, fp.at[b, k], p_recv.at[b, k])
+        acc[b, k] = meet(b, g, fm.at[b, k], fp.at[b, k])
+        if k < 3:
+            dst, recv, d = ((u1, ut_recv, 2), (um, um_recv, 1), (up, up_recv, 3))[k]
+            remote(acc.at[b, k], dst.at[b], p_send.at[b], recv.at[b], rings[b].first(d)).start()
 
     def pieces(b):
         arrive(b, um.at[b], um_recv.at[b])
         arrive(b, up.at[b], up_recv.at[b])
-        total = acc[b, 3] + um[b] + up[b]
+        arrive(b, u1.at[b], ut_recv.at[b])
+        total = acc[b, 3] + um[b] + up[b] + u1[b]
+        here = x * 2 + c
         for s in range(8):
             for j in range(5):
                 stage[b, s, 0:5, 128 * j : 128 * j + 128] = total[40 * j + 5 * s : 40 * j + 5 * s + 5]
@@ -437,23 +445,23 @@
             if s:
                 v = pltpu.roll(v, 128 - 5 * s, 1)
             stage[b, s, 5:7, 0:128] = v[0:2]
-        for k in range(1, 8):
-            s = lax.rem(x * 2 + c + k, 8)
-            remote(
-                stage.at[b, s], fin.at[b, z], f_send.at[b], f_recv.at[b],
-                dev(y, 2 * x + c, lax.div(s, 2), lax.rem(s, 2)),
-            ).start()
-        s = x * 2 + c
-        stay = pltpu.make_async_copy(stage.at[b, s], fin.at[b, z], f_recv.at[b])
-        go = remote(stage.at[b, s], fin.at[b, z], f_send.at[b], f_recv.at[b], dev(y, 2 * x + c, x, c))
-
-        @pl.when(selfish)
-        def _():
-            stay.start()
-
-        @pl.when(jnp.logical_not(selfish))
-        def _():
-            go.start()
+
+            @pl.when(here != s)
+            def _(s=s):
+                remote(
+                    stage.at[b, s], mid.at[b, here], e_send.at[b], e_recv.at[b], dev(y, z, s // 2, s % 2)
+                ).start()
+
+            @pl.when(here == s)
+            def _(s=s):
+                pltpu.make_async_copy(stage.at[b, s], mid.at[b, here], e_recv.at[b]).start()
+
+    def spread_pieces(b):
+        pltpu.make_async_copy(mid.at[b], mid.at[b], e_recv.at[b]).wait()
+        for k in (4, 3, 5, 2, 6, 1, 7):
+            to = lax.rem(z + k, 8)
+            remote(mid.at[b, to], fin.at[b, z], f_send.at[b], f_recv.at[b], dev(y, to, x, c)).start()
+        pltpu.make_async_copy(mid.at[b, z], fin.at[b, z], f_recv.at[b]).start()
 
     sums[...] = jnp.zeros_like(sums)
 
@@ -470,19 +478,17 @@
         sums[0] += eights(d_hid * normed)
         sums[1] += eights(d_hid)
 
-        @pl.when(i == 0)
+        @pl.when(i == 1)
         def _():
             reduce_far(0)
 
         @pl.when(i == 2)
         def _():
-            reduce_near(0, 0)
-            reduce_near(0, 1)
+            reduce_direct(0)
 
         @pl.when(i == 3)
         def _():
-            reduce_near(0, 2)
-            reduce_near(0, 3)
+            reduce_through(0)
 
     top = lax.broadcasted_iota(jnp.int32, (8, 128), 0) == 0
     lane8 = lax.broadcasted_iota(jnp.int32, (8, 128), 1)
@@ -502,38 +508,38 @@
     for k in range(4):
         reduce_first(0, k)
     reduce_far(1)
+    reduce_direct(1)
     pieces(0)
-    for k in range(4):
-        reduce_near(1, k)
+    reduce_through(1)
+    spread_pieces(0)
     for k in range(4):
         reduce_first(1, k)
     pieces(1)
+    pltpu.make_async_copy(fin.at[0], fin.at[0], f_recv.at[0]).wait()
+    out_ref[...] = jnp.sum(fin[0], axis=0)[0:5]
+    spread_pieces(1)
+    pltpu.make_async_copy(fin.at[1], fin.at[1], f_recv.at[1]).wait()
+    total = jnp.sum(fin[1], axis=0)
+    in_ref[...] = total[0:5]
+    gain_ref[...] = total[5:6, 0:5]
+    shift_ref[...] = total[6:7, 0:5]
 
     for b in range(2):
-        pltpu.make_async_copy(fin.at[b], fin.at[b], f_recv.at[b]).wait()
-        o_ref[b] = jnp.sum(fin[b], axis=0)
-
-    @pl.when(mine)
-    def _():
-        pltpu.make_async_copy(rbuf.at[pl.ds(0, 15)], rbuf.at[pl.ds(0, 15)], r_send).wait()
-
-    @pl.when(jnp.logical_not(mine))
-    def _():
-        pltpu.make_async_copy(rbuf, rbuf, r_send).wait()
-
-    for b in range(2):
+
+        @pl.when(mine)
+        def _():
+            pltpu.make_async_copy(rbuf.at[b, pl.ds(0, 15)], rbuf.at[b, pl.ds(0, 15)], r_send.at[b]).wait()
+
+        @pl.when(jnp.logical_not(mine))
+        def _():
+            pltpu.make_async_copy(rbuf.at[b], rbuf.at[b], r_send.at[b]).wait()
+
         pltpu.make_async_copy(wb.at[pl.ds(0, 31)], wb.at[pl.ds(0, 31)], s_send.at[b]).wait()
         pltpu.make_async_copy(sib.at[b], sib.at[b], h_send.at[b]).wait()
         pltpu.make_async_copy(sib.at[b, pl.ds(0, 12)], sib.at[b, pl.ds(0, 12)], q_send.at[b]).wait()
         pltpu.make_async_copy(acc.at[b, pl.ds(0, 3)], acc.at[b, pl.ds(0, 3)], p_send.at[b]).wait()
-
-        @pl.when(selfish)
-        def _():
-            pltpu.make_async_copy(fin.at[b, pl.ds(0, 7)], fin.at[b, pl.ds(0, 7)], f_send.at[b]).wait()
-
-        @pl.when(jnp.logical_not(selfish))
-        def _():
-            pltpu.make_async_copy(fin.at[b], fin.at[b], f_send.at[b]).wait()
+        pltpu.make_async_copy(fin.at[b, pl.ds(0, 7)], fin.at[b, pl.ds(0, 7)], e_send.at[b]).wait()
+        pltpu.make_async_copy(fin.at[b, pl.ds(0, 7)], fin.at[b, pl.ds(0, 7)], f_send.at[b]).wait()
 
 
 def selection():
@@ -567,25 +573,25 @@
     teacher_shift,
     teacher_out,
 ):
-    vecs = jnp.stack([student_gain, student_shift, teacher_gain, teacher_shift]).astype(F32)
-    vecs = jnp.pad(vecs, ((0, 4), (0, 123)))
+    vectors = [v[None, :] for v in (student_gain, student_shift, teacher_gain, teacher_shift)]
     vmem = pl.BlockSpec(memory_space=pltpu.VMEM)
     smem = pl.BlockSpec(memory_space=pltpu.SMEM)
     hbm = pl.BlockSpec(memory_space=pl.ANY)
     half = (208, 128)
     dma = pltpu.SemaphoreType.DMA
-    out = pl.pallas_call(
+    grad_in, grad_out_t, grad_gain, grad_shift = pl.pallas_call(
         kernel,
-        out_shape=jax.ShapeDtypeStruct((2, 8, 640), F32),
-        in_specs=[hbm] * 3 + [smem] * 2 + [vmem] * 7,
-        out_specs=vmem,
+        out_shape=[jax.ShapeDtypeStruct(shape, F32) for shape in ((5, 640), (5, 640), (1, 5), (1, 5))],
+        in_specs=[hbm] * 3 + [smem] * 2 + [vmem] * 10,
+        out_specs=[vmem] * 4,
         scratch_shapes=[
             pltpu.VMEM((1024, 1280), BF16),
             pltpu.VMEM((1024, 1280), BF16),
             pltpu.VMEM((1024, 1280), BF16),
+            pltpu.VMEM((8, 128), F32),
             pltpu.VMEM((2, 64, 128), F32),
             pltpu.VMEM((2, 64, 128), BF16),
-            pltpu.VMEM((16, 64, 128), BF16),
+            pltpu.VMEM((2, 16, 32, 128), BF16),
             pltpu.VMEM((64, 416, 128), BF16),
             pltpu.VMEM((4, 1280, 640), BF16),
             pltpu.VMEM((2, 16, 1280), F32),
@@ -608,9 +614,10 @@
             pltpu.VMEM((2, *half), F32),
             pltpu.VMEM((2, 8, 8, 640), F32),
             pltpu.VMEM((2, 8, 8, 640), F32),
+            pltpu.VMEM((2, 8, 8, 640), F32),
             dma((3,)),
-            dma,
-            dma,
+            dma((2,)),
+            dma((2,)),
             dma((2,)),
             dma((2, 16)),
             dma((2,)),
@@ -620,6 +627,8 @@
             dma((2, 4)),
             dma((2, 4)),
             dma((2, 4)),
+            dma((2,)),
+            dma((2,)),
             dma((2,)),
             dma((2,)),
             dma((2,)),
@@ -630,9 +639,9 @@
         compiler_params=pltpu.CompilerParams(collective_id=0, has_side_effects=True, vmem_limit_bytes=62 * 2**20),
     )(
         features, renoise, critic_grad, student_step, teacher_step, student_in, student_out.T, teacher_in, teacher_out.T,
-        vecs, selection(), membership(),
+        *vectors, selection(), membership(),
     )
-    return out[1, :5], out[0, :5].T, out[1, 5, :5], out[1, 6, :5]
+    return grad_in, grad_out_t.T, grad_gain[0], grad_shift[0]
 
 
 def solution(mesh):

time: 117 us -> 110 us (0.940)
  Pallas kernels: 110 us -> 102 us
  local copies, waits for them, and re-layouts: 2.64 us -> 4.9 us
  other arithmetic: 1.31 us -> 0 us
    pallas_call x1, Pallas kernels: 110 us -> 102 us  [local(): pl.pallas_call(kernel, out_shape=[jax.ShapeDtypeStruct(shape, F32) for sh...]
    unnamed x0 -> x4, local copies, waits for them, and re-layouts: none -> 4.9 us
    transpose x1 -> x0, local copies, waits for them, and re-layouts: 1.36 us -> none  [local(): return (out[1, :5], out[0, :5].T, out[1, 5, :5], out[1, 6, :5])]
    pad x1 -> x0, other arithmetic: 1.31 us -> none  [local(): vecs = jnp.pad(vecs, ((0, 4), (0, 123)))]
    squeeze x1 -> x0, local copies, waits for them, and re-layouts: 1.28 us -> none  [local(): return (out[1, :5], out[0, :5].T, out[1, 5, :5], out[1, 6, :5])]
where the time goes in v3:
time: 110 us; the launch traced here: 109 us
  Pallas kernels  102 us (93%)
  local copies, waits for them, and re-layouts  4.9 us (4%)
  between operations  1.94 us (2%)
    pallas_call x1, Pallas kernels, local(): pl.pallas_call(kernel, out_shape=[jax.ShapeDtypeStruct(shape, F32) for sh...  102 us
    unnamed x4, local copies, waits for them, and re-layouts  4.9 us

profile of v3, /device:TPU:1, one launch (start us, length us, event | category | flops | bytes accessed | tf_op | source)
XLA Modules:
  0.0 109.3 jit_solution(3582502515785597841)
XLA Ops:
  1.9 102.4 %shard_map.174 = (f32[5,640]{1,0:T(8,128)}, f32[5,640]{1,0:T(8,128)}, f32[1,5]{1,0:T(1,128)}, f32[1,5]{1,0:T(1,128)}) custom-call(bf16[1,1024,1280]{2,1,0:T(8,128)(2,1)} %feat_hbm.1, bf16[1,1024,1280]{2,1,0:T(8,128)(2,1)} %noise_hbm.1, bf16[1,1024,1280]{2,1,0:T(8,128)(2,1)} %critic_hbm.1, s32[1]{0:T(128)S(6)} %copy.23.s_step, s32[1]{0:T(128)S(6)} %copy.24.t_step, ...), custom_call_target="tpu_custom_call" | custom-call | tf_op jit(solution)/shard_map/pallas_call | solution.py:582
  104.4 1.3 %copy.25 = f32[5,640]{1,0:T(8,128)} copy(f32[5,640]{1,0:T(8,128)} %get-tuple-element.16) | data formatting | bytes 25600
  105.7 1.3 %copy.26 = f32[640,5]{0,1:T(8,128)} copy(f32[640,5]{0,1:T(8,128)} %bitcast.9) | data formatting | bytes 25600
  107.0 1.1 %copy.27 = f32[5]{0:T(128)} copy(f32[5]{0:T(128)} %bitcast.17) | data formatting | bytes 40
  108.1 1.1 %copy.28 = f32[5]{0:T(128)} copy(f32[5]{0:T(128)} %bitcast.16) | data formatting | bytes 40

commit v4 on v3

--- a/solution.py
+++ b/solution.py
@@ -233,7 +233,7 @@
         remote(at(b, g), at(b, g), s_send.at[b], s_recv.at[b, g], dev(y, z, x, 1 - c)).wait_recv()
 
     row = lax.broadcasted_iota(jnp.int32, (16, 128), 0)
-    for b in range(2):
+    def own_block(b):
         ring = rings[b]
         g = ring.block(0, 0)
         k = (b * 2 + c) * 16 + g
@@ -264,12 +264,14 @@
             send(b, g, ring.second(3))
             hand(b, g)
 
-    def gather_second(b, n, e):
+    def gather_second(b, m):
         ring = rings[b]
-        g = ring.block((0, 3, 1, 2)[n], e)
+        n = m % 4
+        on = 3 if n % 2 == 0 else 1
+        g = ring.block((0, 3, 1, 2)[n], on if m < 4 else 4 - on)
         wait(b, g)
-        if e == (3 if n % 2 == 0 else 1):
-            send(b, g, ring.second(1 if e == 3 else 3))
+        if m < 4:
+            send(b, g, ring.second(4 - on))
         hand(b, g)
 
     def gather_last(b):
@@ -296,11 +298,14 @@
         for n in range(10):
             vec[b, :, 128 * n : 128 * n + 128] = parts[n]
 
+    own_block(0)
+    own_block(1)
     gather_first(0)
+    for m in range(4):
+        gather_second(0, m)
     gather_first(1)
-    for n in range(4):
-        gather_second(0, n, 3)
-        gather_second(0, n, 1)
+    for m in range(4, 8):
+        gather_second(0, m)
     gather_last(0)
     gathered(0)
 
@@ -323,7 +328,7 @@
 
             @pl.when(i == n)
             def _(n=n):
-                gather_second(1, n, 3)
+                gather_second(1, 2 * n)
 
         out = field + lax.dot_general(act[s, :], w[1], nt, preferred_element_type=F32)
         sample[s, :] = out
@@ -334,7 +339,7 @@
 
             @pl.when(i == n)
             def _(n=n):
-                gather_second(1, n, 1)
+                gather_second(1, 2 * n + 1)
 
     gather_last(1)
     mean_to(1)

time: 110 us -> 105 us (0.955)
  Pallas kernels: 102 us -> 97.4 us
    pallas_call x1, Pallas kernels: 102 us -> 97.4 us  [local(): pl.pallas_call(kernel, out_shape=[jax.ShapeDtypeStruct(shape, F32) for sh...]
where the time goes in v4:
time: 105 us; the launch traced here: 104 us
  Pallas kernels  97.4 us (93%)
  local copies, waits for them, and re-layouts  4.9 us (5%)
  between operations  1.94 us (2%)
    pallas_call x1, Pallas kernels, local(): pl.pallas_call(kernel, out_shape=[jax.ShapeDtypeStruct(shape, F32) for sh...  97.4 us
    unnamed x4, local copies, waits for them, and re-layouts  4.9 us

profile of v4, /device:TPU:1, one launch (start us, length us, event | category | flops | bytes accessed | tf_op | source)
XLA Modules:
  0.0 104.2 jit_solution(17262655260877816298)
XLA Ops:
  1.9 97.4 %shard_map.174 = (f32[5,640]{1,0:T(8,128)}, f32[5,640]{1,0:T(8,128)}, f32[1,5]{1,0:T(1,128)}, f32[1,5]{1,0:T(1,128)}) custom-call(bf16[1,1024,1280]{2,1,0:T(8,128)(2,1)} %feat_hbm.1, bf16[1,1024,1280]{2,1,0:T(8,128)(2,1)} %noise_hbm.1, bf16[1,1024,1280]{2,1,0:T(8,128)(2,1)} %critic_hbm.1, s32[1]{0:T(128)S(6)} %copy.23.s_step, s32[1]{0:T(128)S(6)} %copy.24.t_step, ...), custom_call_target="tpu_custom_call" | custom-call | tf_op jit(solution)/shard_map/pallas_call | solution.py:587
  99.3 1.3 %copy.25 = f32[5,640]{1,0:T(8,128)} copy(f32[5,640]{1,0:T(8,128)} %get-tuple-element.16) | data formatting | bytes 25600
  100.7 1.3 %copy.26 = f32[640,5]{0,1:T(8,128)} copy(f32[640,5]{0,1:T(8,128)} %bitcast.9) | data formatting | bytes 25600
  102.0 1.1 %copy.27 = f32[5]{0:T(128)} copy(f32[5]{0:T(128)} %bitcast.17) | data formatting | bytes 40
  103.1 1.1 %copy.28 = f32[5]{0:T(128)} copy(f32[5]{0:T(128)} %bitcast.16) | data formatting | bytes 40

commit v5 on v4

--- a/solution.py
+++ b/solution.py
@@ -131,7 +131,6 @@
     ]
     loads[0].start()
 
-    greet_planes(y, z, x, c)
     for k in range(1, 16):
         signal(dev(y, 2 * x + lax.rem(z + k // 8, 2), lax.rem(x + k // 2, 4), lax.rem(c + k, 2)))
 
@@ -139,6 +138,7 @@
     def _():
         signal(dev(y, 2 * x + lax.rem(z, 2), x, c))
 
+    greet_planes(y, z, x, c)
     for d in (1, 2, 3):
         signal(dev(y, z, lax.rem(x + d, 4), 1 - c))
     for k in range(1, 8):
@@ -182,7 +182,7 @@
         def shard(cc):
             return raw.at[cc, pl.ds(32 * b, 32)]
 
-        for k in range(1, 16):
+        for k in (8, 9, 6, 7, 10, 11, 4, 5, 12, 13, 2, 3, 14, 15, 1):
             cc = lax.rem(c + k, 2)
             remote(
                 shard(cc), rbuf.at[b, slot], r_send.at[b], r_recv.at[b], dev(y, lax.rem(z + k // 2, 8), to_x, cc)

time: 105 us -> 104 us (level)
  no operation moved by 1% of the time
where the time goes in v5:
time: 104 us
  Pallas kernels  96.9 us (93%)
  local copies, waits for them, and re-layouts  4.9 us (5%)
  between operations  1.94 us (2%)
    pallas_call x1, Pallas kernels, local(): pl.pallas_call(kernel, out_shape=[jax.ShapeDtypeStruct(shape, F32) for sh...  96.9 us
    unnamed x4, local copies, waits for them, and re-layouts  4.9 us

profile of v5, /device:TPU:1, one launch (start us, length us, event | category | flops | bytes accessed | tf_op | source)
XLA Modules:
  0.0 103.8 jit_solution(1793610547556054872)
XLA Ops:
  1.9 96.9 %shard_map.174 = (f32[5,640]{1,0:T(8,128)}, f32[5,640]{1,0:T(8,128)}, f32[1,5]{1,0:T(1,128)}, f32[1,5]{1,0:T(1,128)}) custom-call(bf16[1,1024,1280]{2,1,0:T(8,128)(2,1)} %feat_hbm.1, bf16[1,1024,1280]{2,1,0:T(8,128)(2,1)} %noise_hbm.1, bf16[1,1024,1280]{2,1,0:T(8,128)(2,1)} %critic_hbm.1, s32[1]{0:T(128)S(6)} %copy.23.s_step, s32[1]{0:T(128)S(6)} %copy.24.t_step, ...), custom_call_target="tpu_custom_call" | custom-call | tf_op jit(solution)/shard_map/pallas_call | solution.py:587
  98.9 1.3 %copy.25 = f32[5,640]{1,0:T(8,128)} copy(f32[5,640]{1,0:T(8,128)} %get-tuple-element.16) | data formatting | bytes 25600
  100.2 1.3 %copy.26 = f32[640,5]{0,1:T(8,128)} copy(f32[640,5]{0,1:T(8,128)} %bitcast.9) | data formatting | bytes 25600
  101.5 1.1 %copy.27 = f32[5]{0:T(128)} copy(f32[5]{0:T(128)} %bitcast.17) | data formatting | bytes 40
  102.7 1.1 %copy.28 = f32[5]{0:T(128)} copy(f32[5]{0:T(128)} %bitcast.16) | data formatting | bytes 40
